TPU v7x, 32 devices: a whole 2x2x4 slice. The times are simulated.
32 devices in a mesh: wide: 8 (over y, x, core), narrow: 4 (over z).
Axes of the slice: x: 2, y: 2, z: 4, core: 2. Of those that a mesh axis runs over, the one named last changes fastest.
Arguments:
- tracers: float32 [4, 221, 65536], P(None, None, ('wide', 'narrow')), may hold values from -6 to 6
- column_rate: float32 [65536], P(('wide', 'narrow')), may hold values from 0.25 to 2
- loss_rate: float32 [221], replicated, may hold values from 0.05 to 3
- coupling: bfloat16 [221, 221], replicated, may hold values from -0.375 to 0.375
- phys_index: int32 [65536], P(('wide', 'narrow')), may hold values from 0 to 65535, as said below
- iter_count: int32 [65536], P(('wide', 'narrow')), may hold values from 2 to 12, as said below
Outputs:
- updated: float32 [4, 221, 65536], P(None, None, ('wide', 'narrow'))
Inputs may be any that keep to these rules, and one draw needn't show every extreme that they name: A permutation of the columns: column c goes to the device phys_index[c] // 2048 (devices in wide-major order) at slot phys_index[c] % 2048. A device at wide index w sends columns only to devices at wide indices w - 1 to w + 2, with wrap. For each wide step and narrow step (with wrap) every device sends the same number of columns to the device that many steps further on; at most 256, and exactly 256 for some pair of steps. The columns from one device to one device fill a contiguous range of slots. `iter_count`: columns whose physics device lies in 4 consecutive wide indices (with wrap) take 12 // 2 to 12 substeps, the others 2 to 3.
All inputs are finite; a program needn't handle non-finite values.
Results may differ from a plain program's by a relative error of at most 0.00072.
Values sent between devices are 32-bit elements; how exact they have to be, the bound alone decides.
No kernel may reach another device: no remote copies, remote signals or barrier semaphores. Data moves between devices by JAX's collectives and lax.ppermute only.
A program may use at most 128 MiB of HBM per device.

v0:
```python
import functools

import jax
import jax.numpy as jnp
from jax import lax
from jax.experimental import pallas as pl
from jax.experimental.pallas import tpu as pltpu
from jax.sharding import PartitionSpec as P

WIN = 4
LANES = 128
SORT_COLUMNS = 256
INT_ROWS = 256
SEND_ROWS = 32
VMEM = 60 * 1024 * 1024


def from_behind(value, axis, steps):
    count = lax.axis_size(axis)
    pairs = [(source, (source + steps) % count) for source in range(count)]
    return lax.ppermute(value, axis, pairs)


def log2(value):
    bits = value.bit_length() - 1
    assert 1 << bits == value
    return bits


def sort_kernel(sizes, me_ref, phys_ref, rate_ref, count_ref, tracers_ref, rows_ref, table_ref,
                pos_ref, turn_ref, wide_ref, sorted_ref, out_ref, at_ref, total_ref, sem_ref,
                out_sem):
    species, levels, columns, tiles, wide_count, narrow_count, pair_total = sizes
    step = pl.program_id(0)
    lanes = tiles * LANES
    real = species * levels

    @pl.when(step == 0)
    def _():
        phys = phys_ref[...]
        target = lax.shift_right_logical(phys, log2(columns))
        slot = phys & (columns - 1)
        wide_step = (lax.shift_right_logical(target, log2(narrow_count)) - me_ref[0] + 1) & (
            wide_count - 1
        )
        narrow_step = ((target & (narrow_count - 1)) - me_ref[1]) & (narrow_count - 1)
        pair = narrow_step * WIN + wide_step
        member = pair == lax.broadcasted_iota(jnp.int32, (pair_total, columns), 0)
        counts = jnp.sum(jnp.where(member, 1.0, 0.0), axis=1, keepdims=True)
        slot_f = slot.astype(jnp.float32)
        starts = jnp.min(jnp.where(member, slot_f, float(columns)), axis=1, keepdims=True)
        groups = lax.shift_right_logical(counts.astype(jnp.int32) + 7, 3).astype(jnp.float32)
        lane = lax.broadcasted_iota(jnp.int32, (pair_total, LANES), 1)
        row = lax.broadcasted_iota(jnp.int32, (pair_total, LANES), 0)

        def across(value):
            return jnp.sum(jnp.where(lane == row, value, 0.0), axis=0, keepdims=True)

        groups_t = across(groups)
        base = jnp.sum(jnp.where(lane < row, groups_t, 0.0), axis=1, keepdims=True)
        section = row & -WIN
        inner = base - jnp.sum(jnp.where(lane < section, groups_t, 0.0), axis=1, keepdims=True)
        same = (lane & -WIN) == section
        in_step = jnp.sum(jnp.where(same, groups_t, 0.0), axis=1, keepdims=True)
        per = SEND_ROWS // 8
        sections = lax.shift_right_logical(in_step.astype(jnp.int32) + per - 1, log2(per))
        pos = slot_f + jnp.sum(jnp.where(member, base * 8.0 - starts, 0.0), axis=0, keepdims=True)
        pos_ref[...] = pos.astype(jnp.int32)
        copy = pltpu.make_async_copy(pos_ref, at_ref, sem_ref)
        copy.start()
        total_ref[0] = jnp.max(base + groups).astype(jnp.int32)
        for at, value in enumerate((counts, base, inner, sections.astype(jnp.float32))):
            table_ref[at:at + 1, :] = across(value).astype(jnp.int32)
        copy.wait()

    block = tracers_ref.shape[2]
    begin = step * block
    in_group = lax.broadcasted_iota(jnp.int32, (8, LANES), 0)
    for half in range(block // LANES):
        span = slice(half * LANES, (half + 1) * LANES)
        at = pl.ds(pl.multiple_of(begin + half * LANES, LANES), LANES)
        turn_ref[lanes - 16:lanes, :] = jnp.zeros((16, LANES), jnp.float32)
        turn_ref[0:real, :] = tracers_ref[:, :, span].reshape(real, LANES)
        extra = jnp.where(in_group == 5, (phys_ref[:, at] & (columns - 1)).astype(jnp.float32), 0.0)
        extra = jnp.where(in_group == 6, rate_ref[:, at], extra)
        extra = jnp.where(in_group == 7, count_ref[:, at].astype(jnp.float32), extra)
        turn_ref[lanes - 8:lanes, :] = extra
        for tile in range(tiles):
            wide_ref[pl.ds(tile, LANES, stride=8), :] = turn_ref[
                tile * LANES:(tile + 1) * LANES, :
            ].T

        def move(part, carry):
            for extra_row in range(16):
                column = part * 16 + extra_row
                to = pl.multiple_of(at_ref[0, begin + half * LANES + column] * 8, 8)
                sorted_ref[pl.ds(to, 8), :] = wide_ref[pl.ds(pl.multiple_of(column * 8, 8), 8), :]
            return carry

        lax.fori_loop(0, LANES // 16, move, 0)

    @pl.when(step == pl.num_programs(0) - 1)
    def _():
        chunk = 32
        chunks = out_ref.shape[0] // chunk
        for part in range(chunks):
            @pl.when(part * chunk < total_ref[0])
            def _():
                def gather(group, carry):
                    for tile in range(tiles):
                        out_ref[group, tile] = sorted_ref[pl.ds(group * 64 + tile, 8, stride=8), :]
                    return carry

                lax.fori_loop(part * chunk, (part + 1) * chunk, gather, 0)
                here = pl.ds(part * chunk, chunk)
                pltpu.make_async_copy(out_ref.at[here], rows_ref.at[here], out_sem.at[part]).start()
        for part in range(chunks):
            @pl.when(part * chunk < total_ref[0])
            def _():
                here = pl.ds(part * chunk, chunk)
                pltpu.make_async_copy(out_ref.at[here], rows_ref.at[here], out_sem.at[part]).wait()


def integrate_kernel(sizes, total_ref, rows_ref, loss_ref, coupling_ref, out_ref,
                     turn_ref, y_ref, inverse_ref):
    levels, pad, tiles = sizes
    per = LANES // 8
    halves = INT_ROWS // LANES
    lanes = tiles * LANES

    @pl.when(pl.program_id(0) * INT_ROWS < total_ref[0])
    def _():
        for half in range(halves):
            for tile in range(tiles):
                block = rows_ref[half * per:(half + 1) * per, tile].reshape(LANES, LANES)
                turn_ref[half, tile * LANES:(tile + 1) * LANES, :] = block.T
            for level in range(levels):
                y_ref[level * pad:(level + 1) * pad, half * LANES:(half + 1) * LANES] = turn_ref[
                    half, pl.ds(level, pad, stride=levels), :
                ]
        rate = jnp.concatenate(
            [turn_ref[half, lanes - 2:lanes - 1, :] for half in range(halves)], axis=1
        )
        count = jnp.concatenate(
            [turn_ref[half, lanes - 1:lanes, :] for half in range(halves)], axis=1
        )
        step_len = rate / jnp.maximum(count, 1.0)
        inverse_ref[...] = 1.0 / (1.0 + step_len * loss_ref[...])
        last = jnp.max(count).astype(jnp.int32)

        def advance(k, carry):
            active = k.astype(jnp.float32) < count
            for level in range(levels):
                span = slice(level * pad, (level + 1) * pad)
                y = y_ref[span, :]
                squashed = jnp.tanh(y).astype(jnp.bfloat16)
                produced = jnp.dot(
                    coupling_ref[...], squashed, preferred_element_type=jnp.float32
                )
                y_ref[span, :] = jnp.where(
                    active, (y + step_len * produced) * inverse_ref[...], y
                )
            return carry

        lax.fori_loop(0, last, advance, 0)
        for half in range(halves):
            for level in range(levels):
                turn_ref[half, pl.ds(level, pad, stride=levels), :] = y_ref[
                    level * pad:(level + 1) * pad, half * LANES:(half + 1) * LANES
                ]
            for tile in range(tiles):
                block = turn_ref[half, tile * LANES:(tile + 1) * LANES, :]
                out_ref[half * per:(half + 1) * per, tile] = block.T.reshape(per, 8, LANES)


def finish_kernel(sizes, sources, table_ref, *refs):
    species, levels, columns, tiles, room = sizes
    groups = room // 8
    buffers = refs[:-6]
    out_ref, piece_ref, placed_ref, whole_ref, sem_ref, out_sem = refs[-6:]
    copies = []
    for pair, (source, row) in enumerate(sources):
        begin = 0 if row is None else table_ref[row, pair]
        copy = pltpu.make_async_copy(
            buffers[source].at[pl.ds(begin, groups)], piece_ref.at[pair], sem_ref.at[pair]
        )
        copy.start()
        copies.append(copy)
    lane = lax.broadcasted_iota(jnp.int32, (1, LANES), 1)
    in_group = lax.broadcasted_iota(jnp.int32, (8, LANES), 0)
    for pair in range(len(sources)):
        copies[pair].wait()
        count = table_ref[0, pair]
        first = piece_ref[pair, 0, tiles - 1][0:1, :]
        start = jnp.max(jnp.where(lane == LANES - 3, first, 0.0)).astype(jnp.int32)
        start = jnp.clip(start, 0, columns - 1)
        full = lax.shift_right_logical(count, 3)

        def move(group, carry):
            for tile in range(tiles):
                placed_ref[tile, pl.ds(start + group * 8, 8), :] = piece_ref[pair, group, tile]
            return carry

        lax.fori_loop(0, full, move, 0)

        @pl.when((count & 7) > 0)
        def _():
            for tile in range(tiles):
                at = pl.ds(start + full * 8, 8)
                placed_ref[tile, at, :] = jnp.where(
                    in_group < (count & 7), piece_ref[pair, full, tile], placed_ref[tile, at, :]
                )

    per_tile = LANES // levels
    for part in range(columns // LANES):
        at = slice(part * LANES, (part + 1) * LANES)
        for tile in range(tiles):
            block = placed_ref[tile, at, :].T.reshape(per_tile, levels, LANES)
            keep = min(per_tile, species - tile * per_tile)
            whole_ref[tile * per_tile:tile * per_tile + keep, :, at] = block[:keep]
        pltpu.make_async_copy(whole_ref.at[:, :, at], out_ref.at[:, :, at], out_sem.at[part]).start()
    for part in range(columns // LANES):
        at = slice(part * LANES, (part + 1) * LANES)
        pltpu.make_async_copy(whole_ref.at[:, :, at], out_ref.at[:, :, at], out_sem.at[part]).wait()


def tree(index, leaves, *operands):
    def build(low, high):
        if high - low == 1:
            return leaves[low]
        middle = (low + high) // 2
        return lambda at, *rest: lax.cond(
            at < middle, build(low, middle), build(middle, high), at, *rest
        )

    return build(0, len(leaves))(index, *operands)


def local(tracers, column_rate, loss_rate, coupling, phys_index, iter_count):
    levels, species, columns = tracers.shape
    wide_count = lax.axis_size("wide")
    narrow_count = lax.axis_size("narrow")
    pair_total = WIN * narrow_count
    room = 2 * columns // pair_total
    piece = room // 8
    pad = -(-species // 8) * 8
    while levels * pad % LANES or levels * (pad - species) < 8:
        pad += 8
    tiles = levels * pad // LANES
    most = columns + 7 * pair_total + room + SEND_ROWS
    rows_room = -(-most // INT_ROWS) * INT_ROWS
    full = pl.BlockSpec(memory_space=pltpu.VMEM)
    smem = pl.BlockSpec(memory_space=pltpu.SMEM)
    hbm = pl.BlockSpec(memory_space=pl.ANY)
    row_shape = (tiles, 8, LANES)
    rows_type = jax.ShapeDtypeStruct((rows_room // 8,) + row_shape, jnp.float32)

    me = jnp.stack([lax.axis_index("wide"), lax.axis_index("narrow")]).astype(jnp.int32)
    rows, table = pl.pallas_call(
        functools.partial(
            sort_kernel,
            (species, levels, columns, tiles, wide_count, narrow_count, pair_total),
        ),
        grid=(columns // SORT_COLUMNS,),
        in_specs=[smem, full, full, full,
                  pl.BlockSpec((species, levels, SORT_COLUMNS), lambda at: (0, 0, at))],
        out_specs=[hbm, full],
        out_shape=[rows_type, jax.ShapeDtypeStruct((8, LANES), jnp.int32)],
        scratch_shapes=[
            pltpu.VMEM((1, columns), jnp.int32),
            pltpu.VMEM((tiles * LANES, LANES), jnp.float32),
            pltpu.VMEM((LANES * 8, LANES), jnp.float32),
            pltpu.VMEM((rows_room * 8, LANES), jnp.float32),
            pltpu.VMEM((rows_room // 8,) + row_shape, jnp.float32),
            pltpu.SMEM((1, columns), jnp.int32),
            pltpu.SMEM((1,), jnp.int32),
            pltpu.SemaphoreType.DMA(()),
            pltpu.SemaphoreType.DMA((rows_room // INT_ROWS,)),
        ],
        compiler_params=pltpu.CompilerParams(vmem_limit_bytes=VMEM),
        name="sort_columns",
    )(
        me,
        phys_index.reshape(1, columns),
        column_rate.reshape(1, columns),
        iter_count.reshape(1, columns),
        tracers.transpose(1, 0, 2),
    )
    last = narrow_count - 1

    def base(step, at=0):
        return table[1, step * WIN + at]

    def inner(step, at):
        return table[2, step * WIN + at]

    loss_pad = jnp.pad(loss_rate, (0, pad - species)).reshape(pad, 1)
    coupling_pad = jnp.pad(coupling, ((0, pad - species), (0, pad - species)))
    total = (base(last, WIN - 1) * 8 + table[0, pair_total - 1]).reshape(1)
    row_block = pl.BlockSpec((INT_ROWS // 8,) + row_shape, lambda at: (at, 0, 0, 0))
    rows = pl.pallas_call(
        functools.partial(integrate_kernel, (levels, pad, tiles)),
        grid=(rows_room // INT_ROWS,),
        in_specs=[smem, row_block, full, full],
        out_specs=row_block,
        out_shape=rows_type,
        scratch_shapes=[
            pltpu.VMEM((INT_ROWS // LANES, tiles * LANES, LANES), jnp.float32),
            pltpu.VMEM((levels * pad, INT_ROWS), jnp.float32),
            pltpu.VMEM((pad, INT_ROWS), jnp.float32),
        ],
        compiler_params=pltpu.CompilerParams(vmem_limit_bytes=VMEM),
        name="integrate_columns",
    )(total, rows, loss_pad, coupling_pad)

    arrival_room = (WIN + 1) * piece
    send_groups = SEND_ROWS // 8
    most_sections = WIN * room // SEND_ROWS

    def sections_by(step, source, begin, wide_moves):
        operands = [source, begin] + [value for move in wide_moves for value in move[:2]]

        def branch(count, index, source, begin, *moves):
            got = []
            for at, move in enumerate(wide_moves):
                part = lax.dynamic_slice_in_dim(moves[2 * at], moves[2 * at + 1], piece, 0)
                got.append(from_behind(part, "wide", move[2]))
            if count == 0:
                arrived = jnp.zeros((arrival_room,) + row_shape, jnp.float32)
            else:
                part = lax.dynamic_slice_in_dim(source, begin, count * send_groups, 0)
                arrived = from_behind(part, "narrow", step)
                spare = arrival_room - count * send_groups
                arrived = jnp.pad(arrived, ((0, spare), (0, 0), (0, 0), (0, 0)))
            return arrived, got

        leaves = [functools.partial(branch, count) for count in range(most_sections + 1)]
        return tree(table[3, step * WIN], leaves, *operands)

    moving = [at for at in range(WIN) if at != 1]
    order = [narrow_count // 2]
    order += [step for step in range(1, last) if step not in order]
    held = {(1, 0): (rows, 1)}
    zero = jnp.zeros((), jnp.int32)

    wide_moves = [(rows, base(0, at), at - 1) for at in moving]
    wide_moves += [(rows, base(last, at), at - 1) for at in moving]
    previous = None
    for step in order:
        if previous is not None:
            wide_moves = [(arrived, inner(previous, at), at - 1) for at in moving]
        arrived, got = sections_by(step, rows, base(step), wide_moves)
        held[1, step] = (arrived, 2)
        if previous is None:
            for index, at in enumerate(moving):
                held[at, 0] = (got[index], None)
            early = dict(zip(moving, got[len(moving):]))
            early[1] = lax.dynamic_slice_in_dim(rows, base(last, 1), piece, 0)
            merged = jnp.zeros((arrival_room,) + row_shape, jnp.float32)
            for at in range(WIN):
                merged = lax.dynamic_update_slice_in_dim(merged, early[at], inner(last, at), 0)
        else:
            for index, at in enumerate(moving):
                held[at, previous] = (got[index], None)
        previous = step
    wide_moves = [(arrived, inner(previous, at), at - 1) for at in moving]
    arrived, got = sections_by(last, merged, zero, wide_moves)
    for index, at in enumerate(moving):
        held[at, previous] = (got[index], None)
    for at in range(WIN):
        held[at, last] = (arrived, 2)

    buffers, sources = [], []
    for step in range(narrow_count):
        for at in range(WIN):
            value, row = held[at, step]
            known = [index for index, other in enumerate(buffers) if other is value]
            if not known:
                buffers.append(value)
                known = [len(buffers) - 1]
            sources.append((known[0], row))
    updated = pl.pallas_call(
        functools.partial(finish_kernel, (species, levels, columns, tiles, room), tuple(sources)),
        in_specs=[smem] + [hbm] * len(buffers),
        out_specs=hbm,
        out_shape=jax.ShapeDtypeStruct((species, levels, columns), jnp.float32),
        scratch_shapes=[
            pltpu.VMEM((pair_total, piece) + row_shape, jnp.float32),
            pltpu.VMEM((tiles, columns + 8, LANES), jnp.float32),
            pltpu.VMEM((species, levels, columns), jnp.float32),
            pltpu.SemaphoreType.DMA((pair_total,)),
            pltpu.SemaphoreType.DMA((columns // LANES,)),
        ],
        compiler_params=pltpu.CompilerParams(vmem_limit_bytes=VMEM),
        name="place_columns",
    )(table, *buffers)
    return updated.transpose(1, 0, 2)


def solution(mesh):
    placed = (
        P(None, None, ("wide", "narrow")),
        P(("wide", "narrow")),
        P(),
        P(),
        P(("wide", "narrow")),
        P(("wide", "narrow")),
    )
    return jax.shard_map(
        local,
        mesh=mesh,
        in_specs=placed,
        out_specs=P(None, None, ("wide", "narrow")),
        check_vma=False,
    )
```

profile of v0, /device:TPU:0, one launch (start us, length us, event | category | flops | bytes accessed | tf_op | source)
XLA Modules:
  0.0 410.9 jit_solution(3783453706456751512)
XLA Ops:
  3.7 13.4 %sort_columns.1 = (f32[320,7,8,128]{3,2,1,0:T(8,128)}, s32[8,128]{1,0:T(8,128)S(1)}) custom-call(s32[2]{0:T(128)} %pad_add_fusion.me_ref, s32[1,2048]{1,0:T(1,128)} %bitcast.159, f32[1,2048]{1,0:T(1,128)} %bitcast.160, s32[1,2048]{1,0:T(1,128)} %bitcast.161, f32[221,4,2048]{2,1,0:T(4,128)} %bitcast.158), custom_call_target="tpu_custom_call" | custom-call | tf_op jit(solution)/shard_map/sort_columns/pallas_call | solution.py:259
  20.9 45.6 %integrate_columns.1.refs_1_ = f32[320,7,8,128]{3,2,1,0:T(8,128)} custom-call(s32[1]{0:T(128)} %bitcast.153.total_ref, f32[320,7,8,128]{3,2,1,0:T(8,128)} %get-tuple-element.5210.rows_ref, f32[224,1]{1,0:T(8,128)} %copy.7.loss_ref, bf16[224,224]{1,0:T(8,128)(2,1)} %pad.329.coupling_ref), custom_call_target="tpu_custom_call" | custom-call | tf_op jit(solution)/shard_map/integrate_columns/pallas_call | solution.py:301
  66.4 151.1 %conditional.96 = ((f32[160,7,8,128]{3,2,1,0:T(8,128)}, f32[32,7,8,128]{3,2,1,0:T(8,128)}, f32[32,7,8,128]{3,2,1,0:T(8,128)}, f32[32,7,8,128]{3,2,1,0:T(8,128)},...) conditional(s32[]{:T(128)} %convert_element_type.420, (s32[]{:T(128)}, ...), branch_computations={%region_0.33_spmd, %region_33.64_spmd} | conditional | flops 31 | bytes 63308704 | solution.py:232
  67.0 130.2 %conditional.15 = ((f32[160,7,8,128]{3,2,1,0:T(8,128)}, f32[32,7,8,128]{3,2,1,0:T(8,128)}, f32[32,7,8,128]{3,2,1,0:T(8,128)}, f32[32,7,8,128]{3,2,1,0:T(8,128)},...) conditional(s32[]{:T(128)} %convert_element_type.339, (s32[]{:T(128)}, ...), branch_computations={%region_1.17_spmd, %region_18.32_spmd} | conditional | flops 29 | bytes 63308688 | solution.py:232
  77.5 119.6 %conditional.14 = ((f32[160,7,8,128]{3,2,1,0:T(8,128)}, f32[32,7,8,128]{3,2,1,0:T(8,128)}, f32[32,7,8,128]{3,2,1,0:T(8,128)}, f32[32,7,8,128]{3,2,1,0:T(8,128)},...) conditional(s32[]{:T(128)} %convert_element_type.338, (s32[]{:T(128)}, ...), branch_computations={%region_19.24_spmd, %region_26.31_spmd} | conditional | flops 25 | bytes 56083248 | solution.py:232
  78.8 118.4 %conditional.10 = ((f32[160,7,8,128]{3,2,1,0:T(8,128)}, f32[32,7,8,128]{3,2,1,0:T(8,128)}, f32[32,7,8,128]{3,2,1,0:T(8,128)}, f32[32,7,8,128]{3,2,1,0:T(8,128)},...) conditional(s32[]{:T(128)} %convert_element_type.334, (s32[]{:T(128)}, ...), branch_computations={%region_20.20_spmd, %region_23.23_spmd} | conditional | flops 23 | bytes 56083112 | solution.py:232
  79.3 117.8 %conditional.9 = (f32[160,7,8,128]{3,2,1,0:T(8,128)}, f32[32,7,8,128]{3,2,1,0:T(8,128)}, f32[32,7,8,128]{3,2,1,0:T(8,128)}, f32[32,7,8,128]{3,2,1,0:T(8,128)}, f...) conditional(s32[]{:T(128)} %convert_element_type.333, (s32[]{:T(128)}, ...), branch_computations={%region_24.21_spmd, %region_25.22_spmd} | conditional | flops 21 | bytes 54477396 | solution.py:232
  105.7 20.1 %collective-permute-done.90 = f32[32,7,8,128]{3,2,1,0:T(8,128)} collective-permute-done((f32[32,7,8,128]{3,2,1,0:T(8,128)S(1)}, f32[32,7,8,128]{3,2,1,0:T(8,128)}, u32[]{:S(2)}, u32[]{:S(2)}) %collective-permute-start.90) | collective-permute-done | bytes 917536 | tf_op jit(solution)/shard_map/cond/branch_0_fun/cond/branch_1_fun/cond/branch_0_fun/cond/branch_1_fun/cond/branch_1_fun/ppermute | solution.py:21
  125.8 60.4 %collective-permute-done.84 = f32[80,7,8,128]{3,2,1,0:T(8,128)} collective-permute-done((f32[80,7,8,128]{3,2,1,0:T(8,128)S(1)}, f32[80,7,8,128]{3,2,1,0:T(8,128)}, u32[]{:S(2)}, u32[]{:S(2)}) %collective-permute-start.84) | collective-permute-done | bytes 2293792 | tf_op jit(solution)/shard_map/cond/branch_0_fun/cond/branch_1_fun/cond/branch_0_fun/cond/branch_1_fun/cond/branch_1_fun/ppermute | solution.py:21
  217.6 82.6 %conditional.97 = ((f32[160,7,8,128]{3,2,1,0:T(8,128)}, f32[32,7,8,128]{3,2,1,0:T(8,128)}, f32[32,7,8,128]{3,2,1,0:T(8,128)}, f32[32,7,8,128]{3,2,1,0:T(8,128)})) conditional(s32[]{:T(128)} %convert_element_type.422, (s32[]{:T(128)}, s32[8,128]{1,0:T(8,128)}, f32[320,7,8,128]{3,2,1,0:T(8,128)}, f32[160,7,8,128]{3,2,1,0:T(8,128)}) %tuple.1809, ...), branch_computations={%region_64.97_spmd, %region_97.128_spmd} | conditional | flops 22 | bytes 46793320 | solution.py:232
  231.6 59.6 %conditional.61 = ((f32[160,7,8,128]{3,2,1,0:T(8,128)}, f32[32,7,8,128]{3,2,1,0:T(8,128)}, f32[32,7,8,128]{3,2,1,0:T(8,128)}, f32[32,7,8,128]{3,2,1,0:T(8,128)})) conditional(s32[]{:T(128)} %convert_element_type.385, (s32[]{:T(128)}, s32[8,128]{1,0:T(8,128)}, f32[320,7,8,128]{3,2,1,0:T(8,128)}, f32[160,7,8,128]{3,2,1,0:T(8,128)}) %param.127, ...), branch_computations={%region_98.112_spmd, %region_113.127_spmd} | conditional | flops 18 | bytes 33145366 | solution.py:232
  232.3 58.1 %conditional.53 = ((f32[160,7,8,128]{3,2,1,0:T(8,128)}, f32[32,7,8,128]{3,2,1,0:T(8,128)}, f32[32,7,8,128]{3,2,1,0:T(8,128)}, f32[32,7,8,128]{3,2,1,0:T(8,128)})) conditional(s32[]{:T(128)} %convert_element_type.377, (s32[]{:T(128)}, s32[8,128]{1,0:T(8,128)}, f32[320,7,8,128]{3,2,1,0:T(8,128)}, f32[160,7,8,128]{3,2,1,0:T(8,128)}) %param.111, ...), branch_computations={%region_99.104_spmd, %region_106.111_spmd} | conditional | flops 16 | bytes 33145352 | solution.py:232
  234.6 55.9 %conditional.49 = ((f32[160,7,8,128]{3,2,1,0:T(8,128)}, f32[32,7,8,128]{3,2,1,0:T(8,128)}, f32[32,7,8,128]{3,2,1,0:T(8,128)}, f32[32,7,8,128]{3,2,1,0:T(8,128)})) conditional(s32[]{:T(128)} %convert_element_type.373, (s32[]{:T(128)}, s32[]{:T(128)}, f32[320,7,8,128]{3,2,1,0:T(8,128)}, s32[]{:T(128)}, f32[160,7,8,128]{3,2,1,0:T(8,128)}, ...), branch_computations={%region_100.100_spmd, %region_103.103_spmd} | conditional | flops 14 | bytes 33145250 | solution.py:232
  235.3 55.2 %conditional.48 = (f32[160,7,8,128]{3,2,1,0:T(8,128)}, f32[32,7,8,128]{3,2,1,0:T(8,128)}, f32[32,7,8,128]{3,2,1,0:T(8,128)}, f32[32,7,8,128]{3,2,1,0:T(8,128)}) conditional(s32[]{:T(128)} %convert_element_type.372, (s32[]{:T(128)}, f32[320,7,8,128]{3,2,1,0:T(8,128)}, s32[]{:T(128)}, f32[160,7,8,128]{3,2,1,0:T(8,128)}, s32[]{:T(128)}, ...), branch_computations={%region_104.101_spmd, %region_105.102_spmd} | conditional | flops 12 | bytes 31539548 | solution.py:232
  250.8 23.9 %collective-permute-done.306 = f32[52,7,8,128]{3,2,1,0:T(8,128)S(1)} collective-permute-done((f32[52,7,8,128]{3,2,1,0:T(8,128)S(1)}, f32[52,7,8,128]{3,2,1,0:T(8,128)S(1)}, u32[]{:S(2)}, u32[]{:S(2)}) %collective-permute-start.306) | collective-permute-done | bytes 1490976 | tf_op jit(solution)/shard_map/cond/branch_1_fun/cond/branch_0_fun/cond/branch_0_fun/cond/branch_1_fun/cond/branch_0_fun/ppermute | solution.py:21
  277.2 13.2 %collective-permute-done.308 = f32[32,7,8,128]{3,2,1,0:T(8,128)} collective-permute-done((f32[32,7,8,128]{3,2,1,0:T(8,128)S(1)}, f32[32,7,8,128]{3,2,1,0:T(8,128)}, u32[]{:S(2)}, u32[]{:S(2)}) %collective-permute-start.308) | collective-permute-done | bytes 917536 | tf_op jit(solution)/shard_map/cond/branch_1_fun/cond/branch_0_fun/cond/branch_0_fun/cond/branch_1_fun/cond/branch_0_fun/ppermute | solution.py:21
  300.2 100.5 %conditional.98 = ((f32[160,7,8,128]{3,2,1,0:T(8,128)}, f32[32,7,8,128]{3,2,1,0:T(8,128)}, f32[32,7,8,128]{3,2,1,0:T(8,128)}, f32[32,7,8,128]{3,2,1,0:T(8,128)})) conditional(s32[]{:T(128)} %convert_element_type.421, (s32[]{:T(128)}, s32[8,128]{1,0:T(8,128)}, f32[32,7,8,128]{3,2,1,0:T(8,128)}, f32[320,7,8,128]{3,2,1,0:T(8,128)}, ...), branch_computations={%region_128.161_spmd, %region_161.192_spmd} | conditional | flops 34 | bytes 58721032 | solution.py:232
  319.4 79.0 %conditional.92 = ((f32[160,7,8,128]{3,2,1,0:T(8,128)}, f32[32,7,8,128]{3,2,1,0:T(8,128)}, f32[32,7,8,128]{3,2,1,0:T(8,128)}, f32[32,7,8,128]{3,2,1,0:T(8,128)})) conditional(s32[]{:T(128)} %convert_element_type.416, (s32[]{:T(128)}, s32[8,128]{1,0:T(8,128)}, f32[32,7,8,128]{3,2,1,0:T(8,128)}, f32[320,7,8,128]{3,2,1,0:T(8,128)}, ...), branch_computations={%region_162.176_spmd, %region_177.191_spmd} | conditional | flops 30 | bytes 45073088 | solution.py:232
  319.9 77.6 %conditional.84 = ((f32[160,7,8,128]{3,2,1,0:T(8,128)}, f32[32,7,8,128]{3,2,1,0:T(8,128)}, f32[32,7,8,128]{3,2,1,0:T(8,128)}, f32[32,7,8,128]{3,2,1,0:T(8,128)})) conditional(s32[]{:T(128)} %convert_element_type.408, (s32[]{:T(128)}, s32[8,128]{1,0:T(8,128)}, f32[32,7,8,128]{3,2,1,0:T(8,128)}, f32[320,7,8,128]{3,2,1,0:T(8,128)}, ...), branch_computations={%region_163.168_spmd, %region_170.175_spmd} | conditional | flops 28 | bytes 45073076 | solution.py:232
  342.7 54.9 %conditional.80 = ((f32[160,7,8,128]{3,2,1,0:T(8,128)}, f32[32,7,8,128]{3,2,1,0:T(8,128)}, f32[32,7,8,128]{3,2,1,0:T(8,128)}, f32[32,7,8,128]{3,2,1,0:T(8,128)})) conditional(s32[]{:T(128)} %convert_element_type.404, (s32[]{:T(128)}, f32[160,7,8,128]{3,2,1,0:T(8,128)}, s32[]{:T(128)}, f32[160,7,8,128]{3,2,1,0:T(8,128)}, s32[]{:T(128)}, ...), branch_computations={%region_164.164_spmd, %region_167.167_spmd} | conditional | flops 11 | bytes 33145204 | solution.py:232
  343.3 54.3 %conditional.79 = (f32[160,7,8,128]{3,2,1,0:T(8,128)}, f32[32,7,8,128]{3,2,1,0:T(8,128)}, f32[32,7,8,128]{3,2,1,0:T(8,128)}, f32[32,7,8,128]{3,2,1,0:T(8,128)}) conditional(s32[]{:T(128)} %convert_element_type.403, (f32[160,7,8,128]{3,2,1,0:T(8,128)}, s32[]{:T(128)}, f32[160,7,8,128]{3,2,1,0:T(8,128)}, s32[]{:T(128)}, s32[]{:T(128)}) %tuple.1056, ...), branch_computations={%region_168.165_spmd, %region_169.166_spmd} | conditional | flops 9 | bytes 31539510 | solution.py:232
  358.7 19.2 %collective-permute-done.441 = f32[48,7,8,128]{3,2,1,0:T(8,128)S(1)} collective-permute-done((f32[48,7,8,128]{3,2,1,0:T(8,128)S(1)}, f32[48,7,8,128]{3,2,1,0:T(8,128)S(1)}, u32[]{:S(2)}, u32[]{:S(2)}) %collective-permute-start.441) | collective-permute-done | bytes 1376288 | tf_op jit(solution)/shard_map/cond/branch_1_fun/cond/branch_0_fun/cond/branch_0_fun/cond/branch_1_fun/cond/branch_1_fun/ppermute | solution.py:21
  380.3 17.3 %collective-permute-done.443 = f32[32,7,8,128]{3,2,1,0:T(8,128)} collective-permute-done((f32[32,7,8,128]{3,2,1,0:T(8,128)S(1)}, f32[32,7,8,128]{3,2,1,0:T(8,128)}, u32[]{:S(2)}, u32[]{:S(2)}) %collective-permute-start.443) | collective-permute-done | bytes 917536 | tf_op jit(solution)/shard_map/cond/branch_1_fun/cond/branch_0_fun/cond/branch_0_fun/cond/branch_1_fun/cond/branch_1_fun/ppermute | solution.py:21
  400.8 9.6 %place_columns.1 = f32[221,4,2048]{2,1,0:T(4,128)} custom-call(s32[8,128]{1,0:T(8,128)} %copy-done, f32[32,7,8,128]{3,2,1,0:T(8,128)} %get-tuple-element.5211.refs_0_, f32[320,7,8,128]{3,2,1,0:T(8,128)} %integrate_columns.1.refs_1_, f32[32,7,8,128]{3,2,1,0:T(8,128)} %get-tuple-element.5212.refs_2_, f32[32,7,8,128]{3,2,1,0:T(8,128)} %get-tuple-element.5213.refs_3_, ...), custom_call_target="tpu_custom_call" | custom-call | tf_op jit(solution)/shard_map/place_columns/pallas_call | solution.py:382
  (48 shorter events, 66.4 us)
Async XLA Ops:
  17.1 49.3 %copy-start = (s32[8,128]{1,0:T(8,128)}, s32[8,128]{1,0:T(8,128)S(1)}, u32[]{:S(2)}) copy-start(s32[8,128]{1,0:T(8,128)S(1)} %get-tuple-element.5209.table_ref) | copy-start | bytes 12292
  83.0 103.2 %collective-permute-start.84 = (f32[80,7,8,128]{3,2,1,0:T(8,128)S(1)}, f32[80,7,8,128]{3,2,1,0:T(8,128)}, u32[]{:S(2)}, u32[]{:S(2)}) collective-permute-start(f32[80,7,8,128]{3,2,1,0:T(8,128)S(1)} %constant_dynamic-slice_fusion.90), channel_id=1, source_target_pairs={{0,2},{1,3},{2,0},{3,1},{4,6},{5,7},{6,4},{7,5},{8,10},{9,11},{10,... | collective-permute-start | bytes 6881288 | tf_op jit(solution)/shard_map/cond/branch_0_fun/cond/branch_1_fun/cond/branch_0_fun/cond/branch_1_fun/cond/branch_1_fun/ppermute | solution.py:21
  101.5 24.3 %collective-permute-start.90 = (f32[32,7,8,128]{3,2,1,0:T(8,128)S(1)}, f32[32,7,8,128]{3,2,1,0:T(8,128)}, u32[]{:S(2)}, u32[]{:S(2)}) collective-permute-start(f32[32,7,8,128]{3,2,1,0:T(8,128)S(1)} %get-tuple-element.5310), channel_id=1, source_target_pairs={{0,8},{4,12},{8,16},{12,20},{16,24},{20,28},{24,0},{28,4},{1,9},{5... | collective-permute-start | bytes 2752520 | tf_op jit(solution)/shard_map/cond/branch_0_fun/cond/branch_1_fun/cond/branch_0_fun/cond/branch_1_fun/cond/branch_1_fun/ppermute | solution.py:21
  103.0 87.2 %collective-permute-start.89 = (f32[32,7,8,128]{3,2,1,0:T(8,128)S(1)}, f32[32,7,8,128]{3,2,1,0:T(8,128)}, u32[]{:S(2)}, u32[]{:S(2)}) collective-permute-start(f32[32,7,8,128]{3,2,1,0:T(8,128)S(1)} %get-tuple-element.5311), channel_id=1, source_target_pairs={{0,4},{4,8},{8,12},{12,16},{16,20},{20,24},{24,28},{28,0},{1,5},{5... | collective-permute-start | bytes 2752520 | tf_op jit(solution)/shard_map/cond/branch_0_fun/cond/branch_1_fun/cond/branch_0_fun/cond/branch_1_fun/cond/branch_1_fun/ppermute | solution.py:21
  103.0 87.2 %collective-permute-start.88 = (f32[32,7,8,128]{3,2,1,0:T(8,128)S(1)}, f32[32,7,8,128]{3,2,1,0:T(8,128)}, u32[]{:S(2)}, u32[]{:S(2)}) collective-permute-start(f32[32,7,8,128]{3,2,1,0:T(8,128)S(1)} %get-tuple-element.5312), channel_id=1, source_target_pairs={{0,28},{4,0},{8,4},{12,8},{16,12},{20,16},{24,20},{28,24},{1,29},{... | collective-permute-start | bytes 2752520 | tf_op jit(solution)/shard_map/cond/branch_0_fun/cond/branch_1_fun/cond/branch_0_fun/cond/branch_1_fun/cond/branch_1_fun/ppermute | solution.py:21
  105.7 84.6 %collective-permute-start.87 = (f32[32,7,8,128]{3,2,1,0:T(8,128)S(1)}, f32[32,7,8,128]{3,2,1,0:T(8,128)}, u32[]{:S(2)}, u32[]{:S(2)}) collective-permute-start(f32[32,7,8,128]{3,2,1,0:T(8,128)S(1)} %get-tuple-element.5313), channel_id=1, source_target_pairs={{0,8},{4,12},{8,16},{12,20},{16,24},{20,28},{24,0},{28,4},{1,9},{5... | collective-permute-start | bytes 2752520 | tf_op jit(solution)/shard_map/cond/branch_0_fun/cond/branch_1_fun/cond/branch_0_fun/cond/branch_1_fun/cond/branch_1_fun/ppermute | solution.py:21
  125.8 64.5 %collective-permute-start.86 = (f32[32,7,8,128]{3,2,1,0:T(8,128)S(1)}, f32[32,7,8,128]{3,2,1,0:T(8,128)}, u32[]{:S(2)}, u32[]{:S(2)}) collective-permute-start(f32[32,7,8,128]{3,2,1,0:T(8,128)S(1)} %get-tuple-element.5314), channel_id=1, source_target_pairs={{0,4},{4,8},{8,12},{12,16},{16,20},{20,24},{24,28},{28,0},{1,5},{5... | collective-permute-start | bytes 2752520 | tf_op jit(solution)/shard_map/cond/branch_0_fun/cond/branch_1_fun/cond/branch_0_fun/cond/branch_1_fun/cond/branch_1_fun/ppermute | solution.py:21
  186.2 10.9 %collective-permute-start.85 = (f32[32,7,8,128]{3,2,1,0:T(8,128)S(1)}, f32[32,7,8,128]{3,2,1,0:T(8,128)}, u32[]{:S(2)}, u32[]{:S(2)}) collective-permute-start(f32[32,7,8,128]{3,2,1,0:T(8,128)S(1)} %get-tuple-element.5315), channel_id=1, source_target_pairs={{0,28},{4,0},{8,4},{12,8},{16,12},{20,16},{24,20},{28,24},{1,29},{... | collective-permute-start | bytes 2752520 | tf_op jit(solution)/shard_map/cond/branch_0_fun/cond/branch_1_fun/cond/branch_0_fun/cond/branch_1_fun/cond/branch_1_fun/ppermute | solution.py:21
  238.5 36.3 %collective-permute-start.306 = (f32[52,7,8,128]{3,2,1,0:T(8,128)S(1)}, f32[52,7,8,128]{3,2,1,0:T(8,128)S(1)}, u32[]{:S(2)}, u32[]{:S(2)}) collective-permute-start(f32[52,7,8,128]{3,2,1,0:T(8,128)S(1)} %constant_dynamic-slice_fusion.309), channel_id=1, source_target_pairs={{0,1},{1,2},{2,3},{3,0},{4,5},{5,6},{6,7},{7,4},{8,9},{9,10},{10,1... | collective-permute-start | bytes 4472840 | tf_op jit(solution)/shard_map/cond/branch_1_fun/cond/branch_0_fun/cond/branch_0_fun/cond/branch_1_fun/cond/branch_0_fun/ppermute | solution.py:21
  246.5 30.7 %collective-permute-start.309 = (f32[32,7,8,128]{3,2,1,0:T(8,128)S(1)}, f32[32,7,8,128]{3,2,1,0:T(8,128)}, u32[]{:S(2)}, u32[]{:S(2)}) collective-permute-start(f32[32,7,8,128]{3,2,1,0:T(8,128)S(1)} %get-tuple-element.5546), channel_id=1, source_target_pairs={{0,8},{4,12},{8,16},{12,20},{16,24},{20,28},{24,0},{28,4},{1,9},{5... | collective-permute-start | bytes 2752520 | tf_op jit(solution)/shard_map/cond/branch_1_fun/cond/branch_0_fun/cond/branch_0_fun/cond/branch_1_fun/cond/branch_0_fun/ppermute | solution.py:21
  248.2 42.2 %collective-permute-start.308 = (f32[32,7,8,128]{3,2,1,0:T(8,128)S(1)}, f32[32,7,8,128]{3,2,1,0:T(8,128)}, u32[]{:S(2)}, u32[]{:S(2)}) collective-permute-start(f32[32,7,8,128]{3,2,1,0:T(8,128)S(1)} %get-tuple-element.5547), channel_id=1, source_target_pairs={{0,4},{4,8},{8,12},{12,16},{16,20},{20,24},{24,28},{28,0},{1,5},{5... | collective-permute-start | bytes 2752520 | tf_op jit(solution)/shard_map/cond/branch_1_fun/cond/branch_0_fun/cond/branch_0_fun/cond/branch_1_fun/cond/branch_0_fun/ppermute | solution.py:21
  250.4 40.0 %collective-permute-start.307 = (f32[32,7,8,128]{3,2,1,0:T(8,128)S(1)}, f32[32,7,8,128]{3,2,1,0:T(8,128)}, u32[]{:S(2)}, u32[]{:S(2)}) collective-permute-start(f32[32,7,8,128]{3,2,1,0:T(8,128)S(1)} %get-tuple-element.5548), channel_id=1, source_target_pairs={{0,28},{4,0},{8,4},{12,8},{16,12},{20,16},{24,20},{28,24},{1,29},{... | collective-permute-start | bytes 2752520 | tf_op jit(solution)/shard_map/cond/branch_1_fun/cond/branch_0_fun/cond/branch_0_fun/cond/branch_1_fun/cond/branch_0_fun/ppermute | solution.py:21
  344.7 33.2 %collective-permute-start.441 = (f32[48,7,8,128]{3,2,1,0:T(8,128)S(1)}, f32[48,7,8,128]{3,2,1,0:T(8,128)S(1)}, u32[]{:S(2)}, u32[]{:S(2)}) collective-permute-start(f32[48,7,8,128]{3,2,1,0:T(8,128)S(1)} %dynamic_slice.1466), channel_id=1, source_target_pairs={{0,3},{1,0},{2,1},{3,2},{4,7},{5,4},{6,5},{7,6},{8,11},{9,8},{10,9... | collective-permute-start | bytes 4128776 | tf_op jit(solution)/shard_map/cond/branch_1_fun/cond/branch_0_fun/cond/branch_0_fun/cond/branch_1_fun/cond/branch_1_fun/ppermute | solution.py:21
  355.4 24.9 %collective-permute-start.444 = (f32[32,7,8,128]{3,2,1,0:T(8,128)S(1)}, f32[32,7,8,128]{3,2,1,0:T(8,128)}, u32[]{:S(2)}, u32[]{:S(2)}) collective-permute-start(f32[32,7,8,128]{3,2,1,0:T(8,128)S(1)} %get-tuple-element.5696), channel_id=1, source_target_pairs={{0,8},{4,12},{8,16},{12,20},{16,24},{20,28},{24,0},{28,4},{1,9},{5... | collective-permute-start | bytes 2752520 | tf_op jit(solution)/shard_map/cond/branch_1_fun/cond/branch_0_fun/cond/branch_0_fun/cond/branch_1_fun/cond/branch_1_fun/ppermute | solution.py:21
  356.1 41.5 %collective-permute-start.443 = (f32[32,7,8,128]{3,2,1,0:T(8,128)S(1)}, f32[32,7,8,128]{3,2,1,0:T(8,128)}, u32[]{:S(2)}, u32[]{:S(2)}) collective-permute-start(f32[32,7,8,128]{3,2,1,0:T(8,128)S(1)} %get-tuple-element.5697), channel_id=1, source_target_pairs={{0,4},{4,8},{8,12},{12,16},{16,20},{20,24},{24,28},{28,0},{1,5},{5... | collective-permute-start | bytes 2752520 | tf_op jit(solution)/shard_map/cond/branch_1_fun/cond/branch_0_fun/cond/branch_0_fun/cond/branch_1_fun/cond/branch_1_fun/ppermute | solution.py:21
  356.1 41.5 %collective-permute-start.442 = (f32[32,7,8,128]{3,2,1,0:T(8,128)S(1)}, f32[32,7,8,128]{3,2,1,0:T(8,128)}, u32[]{:S(2)}, u32[]{:S(2)}) collective-permute-start(f32[32,7,8,128]{3,2,1,0:T(8,128)S(1)} %get-tuple-element.5698), channel_id=1, source_target_pairs={{0,28},{4,0},{8,4},{12,8},{16,12},{20,16},{24,20},{28,24},{1,29},{... | collective-permute-start | bytes 2752520 | tf_op jit(solution)/shard_map/cond/branch_1_fun/cond/branch_0_fun/cond/branch_0_fun/cond/branch_1_fun/cond/branch_1_fun/ppermute | solution.py:21
where the time goes:
time: 405 us; the launch traced here: 411 us
  waiting for transfers between devices  161 us (40%)
  loops' own time  118 us (29%)
  Pallas kernels  68.6 us (17%)
  local copies, waits for them, and re-layouts  39 us (10%)
  starting transfers between devices  19.9 us (5%)
    ppermute x15, waiting for transfers between devices, from_behind(): return lax.ppermute(value, axis, pairs)  161 us
    another operation x15, loops' own time, build(): lax.cond(at < middle, build(low, middle), build(middle, high), at, *rest)  118 us
    pallas_call x1, Pallas kernels, local(): pl.pallas_call(functools.partial(integrate_kernel, (levels, pad, tiles)),...  45.6 us
    ppermute x15, starting transfers between devices, from_behind(): return lax.ppermute(value, axis, pairs)  19.9 us
    pallas_call x1, Pallas kernels, local(): pl.pallas_call(functools.partial(sort_kernel, (species, levels, columns,...  13.4 us
    pallas_call x1, Pallas kernels, local(): pl.pallas_call(functools.partial(finish_kernel, (species, levels, columns...  9.62 us
    pad x3, local copies, waits for them, and re-layouts, branch(): arrived = jnp.pad(arrived, ((0, spare), (0, 0), (0, 0), (0, 0)))  8.8 us
    dynamic_update_slice x4, local copies, waits for them, and re-layouts, local(): lax.dynamic_update_slice_in_dim(merged, early[at], inner(last, at), 0)  8.64 us
  transfers between devices with their start and end apart: 15, of which 7 were waited for; matrix products, arithmetic and copies ran while one was open for 4% of the time, Pallas kernels for 0%

commit v1 on v0

v1 whole, which is shorter than its diff:
```python
import functools

import jax
import jax.numpy as jnp
from jax import lax
from jax.experimental import pallas as pl
from jax.experimental.pallas import tpu as pltpu
from jax.sharding import PartitionSpec as P

WIN = 4
MAXIT = 12
LANES = 128
SORT_COLUMNS = 256
INT_ROWS = 256
UNIT = 4
VMEM = 60 * 1024 * 1024


def from_behind(value, axis, steps):
    count = lax.axis_size(axis)
    pairs = [(source, (source + steps) % count) for source in range(count)]
    return lax.ppermute(value, axis, pairs)


def log2(value):
    bits = value.bit_length() - 1
    assert 1 << bits == value
    return bits


def sort_kernel(sizes, me_ref, phys_ref, rate_ref, count_ref, tracers_ref, rows_ref, table_ref,
                *rest):
    species, levels, columns, tiles, wide_count, narrow_count, pair_total = sizes[:7]
    cuts = sizes[7]
    cut_refs, scratch = rest[:len(cuts)], rest[len(cuts):]
    (pos_ref, turn_ref, wide_ref, sorted_ref, out_ref, at_ref, table_smem, sem_ref,
     out_sem) = scratch
    step = pl.program_id(0)
    lanes = tiles * LANES
    real = species * levels

    @pl.when(step == 0)
    def _():
        phys = phys_ref[...]
        target = lax.shift_right_logical(phys, log2(columns))
        slot = phys & (columns - 1)
        wide_step = (lax.shift_right_logical(target, log2(narrow_count)) - me_ref[0] + 1) & (
            wide_count - 1
        )
        narrow_step = ((target & (narrow_count - 1)) - me_ref[1]) & (narrow_count - 1)
        pair = narrow_step * WIN + wide_step
        member = pair == lax.broadcasted_iota(jnp.int32, (pair_total, columns), 0)
        counts = jnp.sum(jnp.where(member, 1.0, 0.0), axis=1, keepdims=True)
        slot_f = slot.astype(jnp.float32)
        starts = jnp.min(jnp.where(member, slot_f, float(columns)), axis=1, keepdims=True)
        groups = lax.shift_right_logical(counts.astype(jnp.int32) + 7, 3).astype(jnp.float32)
        lane = lax.broadcasted_iota(jnp.int32, (pair_total, LANES), 1)
        row = lax.broadcasted_iota(jnp.int32, (pair_total, LANES), 0)

        def across(value):
            return jnp.sum(jnp.where(lane == row, value, 0.0), axis=0, keepdims=True)

        groups_t = across(groups)
        base = jnp.sum(jnp.where(lane < row, groups_t, 0.0), axis=1, keepdims=True)
        section = row & -WIN
        inner = base - jnp.sum(jnp.where(lane < section, groups_t, 0.0), axis=1, keepdims=True)
        same = (lane & -WIN) == section
        in_step = jnp.sum(jnp.where(same, groups_t, 0.0), axis=1, keepdims=True)
        pos = slot_f + jnp.sum(jnp.where(member, base * 8.0 - starts, 0.0), axis=0, keepdims=True)
        pos_ref[...] = pos.astype(jnp.int32)
        copy = pltpu.make_async_copy(pos_ref, at_ref, sem_ref)
        copy.start()
        table_ref[...] = jnp.zeros_like(table_ref)
        for at, value in enumerate((counts, base, inner, in_step)):
            table_ref[at:at + 1, :] = across(value).astype(jnp.int32)
        copy.wait()
        copy = pltpu.make_async_copy(table_ref, table_smem, sem_ref)
        copy.start()
        copy.wait()

    block = tracers_ref.shape[2]
    begin = step * block
    in_group = lax.broadcasted_iota(jnp.int32, (8, LANES), 0)
    for half in range(block // LANES):
        span = slice(half * LANES, (half + 1) * LANES)
        at = pl.ds(pl.multiple_of(begin + half * LANES, LANES), LANES)
        turn_ref[lanes - 16:lanes, :] = jnp.zeros((16, LANES), jnp.float32)
        turn_ref[0:real, :] = tracers_ref[:, :, span].reshape(real, LANES)
        extra = jnp.where(in_group == 5, (phys_ref[:, at] & (columns - 1)).astype(jnp.float32), 0.0)
        extra = jnp.where(in_group == 6, rate_ref[:, at], extra)
        extra = jnp.where(in_group == 7, count_ref[:, at].astype(jnp.float32), extra)
        turn_ref[lanes - 8:lanes, :] = extra
        for tile in range(tiles):
            wide_ref[pl.ds(tile, LANES, stride=8), :] = turn_ref[
                tile * LANES:(tile + 1) * LANES, :
            ].T

        def move(part, carry):
            for extra_row in range(16):
                column = part * 16 + extra_row
                to = pl.multiple_of(at_ref[0, begin + half * LANES + column] * 8, 8)
                sorted_ref[pl.ds(to, 8), :] = wide_ref[pl.ds(pl.multiple_of(column * 8, 8), 8), :]
            return carry

        lax.fori_loop(0, LANES // 16, move, 0)

    @pl.when(step == pl.num_programs(0) - 1)
    def _():
        chunk = 32
        chunks = out_ref.shape[0] // chunk
        total = table_smem[1, pair_total - 1] + table_smem[0, pair_total - 1]
        for part in range(chunks):
            @pl.when(part * chunk < total)
            def _():
                def gather(group, carry):
                    for tile in range(tiles):
                        out_ref[group, tile] = sorted_ref[pl.ds(group * 64 + tile, 8, stride=8), :]
                    return carry

                lax.fori_loop(part * chunk, (part + 1) * chunk, gather, 0)

        copies = [pltpu.make_async_copy(out_ref, rows_ref.at[pl.ds(0, out_ref.shape[0])],
                                        out_sem.at[len(cuts)])]
        for index, (begin, size) in enumerate(cuts):
            begin = jnp.minimum(begin(table_smem), out_ref.shape[0] - size)
            copies.append(pltpu.make_async_copy(
                out_ref.at[pl.ds(begin, size)], cut_refs[index], out_sem.at[index]
            ))
        for copy in copies:
            copy.start()
        for copy in copies:
            copy.wait()


def chunk_sizes(static):
    units = static // UNIT
    return [UNIT] + [UNIT << bit for bit in reversed(range(log2(units)))]


def units_over(in_step, static):
    return lax.shift_right_logical(jnp.maximum(in_step - static, 0) + UNIT - 1, log2(UNIT))


def chunk_places(in_step, static):
    units = units_over(in_step, static)
    rest = jnp.maximum(units - 1, 0)
    places = [(units > 0, jnp.int32(static))]
    begin = static + UNIT
    for size in chunk_sizes(static)[1:]:
        digit = lax.shift_right_logical(rest, log2(size // UNIT)) & 1
        places.append((digit > 0, begin))
        begin = begin + digit * size
    return places


def start_arrival(refs, sems, room_ref, in_step, static, first):
    copy = pltpu.make_async_copy(refs[0], room_ref.at[pl.ds(first, static)], sems(0))
    copy.start()
    waits = [(None, copy)]
    places = chunk_places(in_step, static)
    for index, (wanted, begin) in enumerate(places):
        size = chunk_sizes(static)[index]
        copy = pltpu.make_async_copy(
            refs[1 + index], room_ref.at[pl.ds(first + begin, size)], sems(1 + index)
        )
        pl.when(wanted)(copy.start)
        waits.append((wanted, copy))
    return waits


def wait_all(waits):
    for wanted, copy in waits:
        if wanted is None:
            copy.wait()
        else:
            pl.when(wanted)(copy.wait)


def integrate_block(sizes, room_ref, first, valid, loss_ref, coupling_ref,
                    turn_ref, y_ref, inverse_ref):
    levels, pad, tiles = sizes
    per = LANES // 8
    halves = INT_ROWS // LANES
    lanes = tiles * LANES
    for half in range(halves):
        begin = first + half * per
        for tile in range(tiles):
            block = room_ref[pl.ds(begin, per), tile].reshape(LANES, LANES)
            turn_ref[half, tile * LANES:(tile + 1) * LANES, :] = block.T
        for level in range(levels):
            y_ref[level, :, half * LANES:(half + 1) * LANES] = turn_ref[
                half, pl.ds(level, pad, stride=levels), :
            ]
    rate = jnp.concatenate(
        [turn_ref[half, lanes - 2:lanes - 1, :] for half in range(halves)], axis=1
    )
    count = jnp.concatenate(
        [turn_ref[half, lanes - 1:lanes, :] for half in range(halves)], axis=1
    )
    lane = lax.broadcasted_iota(jnp.int32, (1, INT_ROWS), 1)
    count = jnp.where((lane < valid) & (count <= MAXIT), count, 0.0)
    step_len = rate / jnp.maximum(count, 1.0)
    inverse_ref[...] = 1.0 / (1.0 + step_len * loss_ref[...])
    last = jnp.max(count).astype(jnp.int32)

    def advance(k, carry):
        active = k.astype(jnp.float32) < count

        def one_level(level, inner):
            y = y_ref[level]
            squashed = jnp.tanh(y).astype(jnp.bfloat16)
            produced = jnp.dot(coupling_ref[...], squashed, preferred_element_type=jnp.float32)
            y_ref[level] = jnp.where(active, (y + step_len * produced) * inverse_ref[...], y)
            return inner

        for level in range(levels):
            one_level(level, 0)
        return carry

    lax.fori_loop(0, last, advance, 0)
    for half in range(halves):
        begin = first + half * per
        for level in range(levels):
            turn_ref[half, pl.ds(level, pad, stride=levels), :] = y_ref[
                level, :, half * LANES:(half + 1) * LANES
            ]
        for tile in range(tiles):
            block = turn_ref[half, tile * LANES:(tile + 1) * LANES, :]
            room_ref[pl.ds(begin, per), tile] = block.T.reshape(per, 8, LANES)


def integrate_kernel(sizes, plan, table_ref, loss_ref, coupling_ref, *refs):
    loads, merges, blocks, stores, operands = plan
    sources = refs[:operands]
    results = refs[operands:operands + len(stores)]
    room_ref, turn_ref, y_ref, inverse_ref, rows_ref, sem_ref, out_sem = refs[
        operands + len(stores):
    ]
    copies = []
    for index, (source, begin, groups, to) in enumerate(loads):
        ref = sources[source]
        if begin is not None:
            ref = ref.at[pl.ds(begin(table_ref), groups)]
        copies.append(
            pltpu.make_async_copy(ref, room_ref.at[pl.ds(to, groups)], sem_ref.at[index])
        )
    for copy in copies:
        copy.start()
    for copy in copies:
        copy.wait()
    for begin, groups, to in merges:
        to = to(table_ref)

        def move(group, carry):
            room_ref[to + group] = room_ref[begin + group]
            return carry

        lax.fori_loop(0, groups(table_ref), move, 0)
    for index, (begin, rows) in enumerate(blocks):
        rows_ref[0, index] = jnp.int32(begin)
        rows_ref[1, index] = rows(table_ref)

    def one_block(index, carry):
        valid = rows_ref[1, index]

        @pl.when(valid > 0)
        def _():
            integrate_block(sizes, room_ref, rows_ref[0, index], valid, loss_ref, coupling_ref,
                            turn_ref, y_ref, inverse_ref)

        return carry

    lax.fori_loop(0, len(blocks), one_block, 0)
    copies = []
    for index, (begin, groups) in enumerate(stores):
        copies.append(pltpu.make_async_copy(
            room_ref.at[pl.ds(begin(table_ref), groups)], results[index], out_sem.at[index]
        ))
    for copy in copies:
        copy.start()
    for copy in copies:
        copy.wait()


def cut_kernel(static, step, table_ref, *refs):
    arrived = len(chunk_sizes(static)) + 1
    pieces = refs[arrived:arrived + WIN]
    room_ref, sem_ref, out_sem = refs[arrived + WIN:]
    wait_all(start_arrival(refs[:arrived], lambda at: sem_ref.at[at], room_ref,
                           table_ref[3, step * WIN], static, 0))
    copies = []
    for at in range(WIN):
        begin = table_ref[2, step * WIN + at]
        copies.append(pltpu.make_async_copy(
            room_ref.at[pl.ds(begin, pieces[at].shape[0])], pieces[at], out_sem.at[at]
        ))
    for copy in copies:
        copy.start()
    for copy in copies:
        copy.wait()


def finish_kernel(sizes, table_ref, *refs):
    species, levels, columns, tiles, static, narrow_count = sizes
    arrived = len(chunk_sizes(static)) + 1
    pair_total = narrow_count * WIN
    whole_pieces = pair_total - WIN
    out_ref, piece_ref, room_ref, placed_ref, whole_ref, sem_ref, out_sem = refs[-7:]
    copies = []
    for pair in range(whole_pieces):
        copies.append(pltpu.make_async_copy(refs[pair], piece_ref.at[pair], sem_ref.at[pair]))
        copies[-1].start()
    waits = start_arrival(refs[whole_pieces:whole_pieces + arrived],
                          lambda at: sem_ref.at[whole_pieces + at], room_ref,
                          table_ref[3, whole_pieces], static, 0)
    lane = lax.broadcasted_iota(jnp.int32, (1, LANES), 1)
    in_group = lax.broadcasted_iota(jnp.int32, (8, LANES), 0)
    for pair in range(pair_total):
        if pair < whole_pieces:
            copies[pair].wait()
            piece = piece_ref.at[pair]
            begin = 0
        else:
            if pair == whole_pieces:
                wait_all(waits)
            piece = room_ref
            begin = table_ref[2, pair]
        count = table_ref[0, pair]
        first = piece[begin, tiles - 1][0:1, :]
        start = jnp.max(jnp.where(lane == LANES - 3, first, 0.0)).astype(jnp.int32)
        start = jnp.clip(start, 0, columns - 1)
        full = lax.shift_right_logical(count, 3)

        def move(group, carry):
            for tile in range(tiles):
                placed_ref[tile, pl.ds(start + group * 8, 8), :] = piece[begin + group, tile]
            return carry

        lax.fori_loop(0, full, move, 0)

        @pl.when((count & 7) > 0)
        def _():
            for tile in range(tiles):
                at = pl.ds(start + full * 8, 8)
                placed_ref[tile, at, :] = jnp.where(
                    in_group < (count & 7), piece[begin + full, tile], placed_ref[tile, at, :]
                )

    per_tile = LANES // levels
    for part in range(columns // LANES):
        at = slice(part * LANES, (part + 1) * LANES)
        for tile in range(tiles):
            block = placed_ref[tile, at, :].T.reshape(per_tile, levels, LANES)
            keep = min(per_tile, species - tile * per_tile)
            whole_ref[tile * per_tile:tile * per_tile + keep, :, at] = block[:keep]
        pltpu.make_async_copy(whole_ref.at[:, :, at], out_ref.at[:, :, at], out_sem.at[part]).start()
    for part in range(columns // LANES):
        at = slice(part * LANES, (part + 1) * LANES)
        pltpu.make_async_copy(whole_ref.at[:, :, at], out_ref.at[:, :, at], out_sem.at[part]).wait()


def local(tracers, column_rate, loss_rate, coupling, phys_index, iter_count):
    levels, species, columns = tracers.shape
    wide_count = lax.axis_size("wide")
    narrow_count = lax.axis_size("narrow")
    pair_total = WIN * narrow_count
    room = 2 * columns // pair_total
    piece = room // 8
    pad = -(-species // 8) * 8
    while levels * pad % LANES or levels * (pad - species) < 8:
        pad += 8
    tiles = levels * pad // LANES
    static = columns // narrow_count // 8
    sizes = chunk_sizes(static)
    most = columns + 7 * pair_total + UNIT * 8
    sort_room = -(-max(most, columns + 7 * pair_total + room) // INT_ROWS) * INT_ROWS
    rows_room = sort_room // 8 + 2 * static
    full = pl.BlockSpec(memory_space=pltpu.VMEM)
    smem = pl.BlockSpec(memory_space=pltpu.SMEM)
    hbm = pl.BlockSpec(memory_space=pl.ANY)
    row_shape = (tiles, 8, LANES)
    last = narrow_count - 1
    moving = [at for at in range(WIN) if at != 1]
    order = [narrow_count // 2]
    order += [step for step in range(1, last) if step not in order] + [last]
    params = pltpu.CompilerParams(vmem_limit_bytes=VMEM)

    def rows_type(groups):
        return jax.ShapeDtypeStruct((groups,) + row_shape, jnp.float32)

    def entry(row, step, at=0):
        return lambda table: table[row, step * WIN + at]

    def group_cuts(begin, in_step):
        cuts = [(begin, static)]
        for index, size in enumerate(sizes):
            cuts.append((
                lambda table, index=index: begin(table)
                + chunk_places(in_step(table), static)[index][1],
                size,
            ))
        return cuts

    cuts = group_cuts(entry(1, order[0]), entry(3, order[0]))
    cuts += [(entry(1, 0, at), piece) for at in moving]
    cuts += [(entry(1, last, at), piece) for at in moving]
    me = jnp.stack([lax.axis_index("wide"), lax.axis_index("narrow")]).astype(jnp.int32)
    rows, table, *first = pl.pallas_call(
        functools.partial(
            sort_kernel,
            (species, levels, columns, tiles, wide_count, narrow_count, pair_total, cuts),
        ),
        grid=(columns // SORT_COLUMNS,),
        in_specs=[smem, full, full, full,
                  pl.BlockSpec((species, levels, SORT_COLUMNS), lambda at: (0, 0, at))],
        out_specs=[hbm, full] + [hbm] * len(cuts),
        out_shape=[rows_type(rows_room), jax.ShapeDtypeStruct((8, LANES), jnp.int32)]
        + [rows_type(size) for _, size in cuts],
        scratch_shapes=[
            pltpu.VMEM((1, columns), jnp.int32),
            pltpu.VMEM((tiles * LANES, LANES), jnp.float32),
            pltpu.VMEM((LANES * 8, LANES), jnp.float32),
            pltpu.VMEM((sort_room * 8, LANES), jnp.float32),
            pltpu.VMEM((sort_room // 8,) + row_shape, jnp.float32),
            pltpu.SMEM((1, columns), jnp.int32),
            pltpu.SMEM((8, LANES), jnp.int32),
            pltpu.SemaphoreType.DMA(()),
            pltpu.SemaphoreType.DMA((len(cuts) + 1,)),
        ],
        compiler_params=params,
        name="sort_columns",
    )(
        me,
        phys_index.reshape(1, columns),
        column_rate.reshape(1, columns),
        iter_count.reshape(1, columns),
        tracers.transpose(1, 0, 2),
    )
    loss_pad = jnp.pad(loss_rate, (0, pad - species)).reshape(pad, 1)
    coupling_pad = jnp.pad(coupling, ((0, pad - species), (0, pad - species)))
    block = INT_ROWS // 8

    def integrate(operands, loads, merges, blocks, stores):
        groups = max([to + size for _, _, size, to in loads] + [begin + block for begin, _ in blocks])
        groups += static
        flops = 2 * levels * pad * pad * 6 * INT_ROWS * len(blocks)
        return pl.pallas_call(
            functools.partial(
                integrate_kernel, (levels, pad, tiles),
                (loads, merges, blocks, stores, len(operands)),
            ),
            in_specs=[smem, full, full] + [hbm] * len(operands),
            out_specs=[hbm] * len(stores),
            out_shape=[rows_type(size) for _, size in stores],
            scratch_shapes=[
                pltpu.VMEM((groups,) + row_shape, jnp.float32),
                pltpu.VMEM((INT_ROWS // LANES, tiles * LANES, LANES), jnp.float32),
                pltpu.VMEM((levels, pad, INT_ROWS), jnp.float32),
                pltpu.VMEM((pad, INT_ROWS), jnp.float32),
                pltpu.SMEM((2, LANES), jnp.int32),
                pltpu.SemaphoreType.DMA((len(loads),)),
                pltpu.SemaphoreType.DMA((len(stores),)),
            ],
            compiler_params=params,
            cost_estimate=pl.CostEstimate(
                flops=flops, bytes_accessed=8 * groups * 8 * tiles * LANES,
                transcendentals=flops // (2 * pad),
            ),
            name="integrate_columns",
        )(table, loss_pad, coupling_pad, *operands)

    def rows_of(step, at=0):
        return entry(0, step, at)

    def group_blocks(begin, step):
        return [
            (begin + part * block,
             lambda table, part=part: table[3, step * WIN] * 8 - part * INT_ROWS)
            for part in range(2 * static // block)
        ]

    def here(begin):
        return lambda table: jnp.int32(begin)

    def step_over(step, parts):
        def leaf(units, *parts):
            taken = [units > 0]
            taken += [(units - 1) // (size // UNIT) % 2 == 1 and units > 0 for size in sizes[1:]]
            return [
                from_behind(part, "narrow", step) if sent else jnp.zeros_like(part)
                for part, sent in zip(parts, taken)
            ]

        leaves = [functools.partial(leaf, units) for units in range(static // UNIT + 1)]
        return lax.switch(units_over(table[3, step * WIN], static), leaves, *parts)

    pieces = {}
    outgoing = first[:len(sizes) + 1]
    wide_now = list(first[len(sizes) + 1:])
    keys_now = [(at, 0) for at in moving] + [(at, last) for at in moving]
    for phase, step in enumerate(order):
        static_part = from_behind(outgoing[0], "narrow", step)
        wide_got = [
            from_behind(value, "wide", key[0] - 1) for value, key in zip(wide_now, keys_now)
        ]
        operands, loads, merges, blocks, stores, named = [], [], [], [], [], []
        used = 0
        if phase + 1 < len(order):
            coming = order[phase + 1]
            if coming == last:
                operands += [pieces[at, last] for at in moving] + [rows]
                for index, at in enumerate(moving):
                    loads.append((index, None, piece, 2 * static + at * piece))
                loads.append((len(moving), entry(1, last, 1), piece, 2 * static + piece))
                for at in range(WIN):
                    merges.append((2 * static + at * piece, lambda table, at=at: (
                        lax.shift_right_logical(table[0, last * WIN + at] + 7, 3)
                    ), entry(2, last, at)))
                used = 2 * static + WIN * piece
            else:
                operands.append(rows)
                loads.append((0, entry(1, coming), 2 * static, 0))
                used = 2 * static
            blocks += group_blocks(0, coming)
            stores += group_cuts(here(0), entry(3, coming))
        extra = []
        if phase == 0:
            extra.append(((1, 0), None))
        if phase == 1:
            extra += [((at, 0), pieces[at, 0]) for at in moving]
        if phase == 2:
            extra += [((at, order[0]), pieces[at, order[0]]) for at in range(WIN)]
        used = -(-used // block) * block
        for key, value in extra:
            if value is None:
                loads.append((operands.index(rows), entry(1, key[1], key[0]), piece, used))
            else:
                operands.append(value)
                loads.append((len(operands) - 1, None, piece, used))
            blocks.append((used, rows_of(key[1], key[0])))
            stores.append((here(used), piece))
            named.append(key)
            used += block
        if stores:
            results = integrate(operands, loads, merges, blocks, stores)
            done = dict(zip(named, results[len(results) - len(named):]))
        over = step_over(step, outgoing[1:])
        pieces.update(zip(keys_now, wide_got))
        if stores:
            pieces.update(done)
            outgoing = results[:len(results) - len(named)]
        arrived = [static_part] + list(over)
        if step != last:
            cut = pl.pallas_call(
                functools.partial(cut_kernel, static, step),
                in_specs=[smem] + [hbm] * len(arrived),
                out_specs=[hbm] * WIN,
                out_shape=[rows_type(piece)] * WIN,
                scratch_shapes=[
                    pltpu.VMEM((3 * static,) + row_shape, jnp.float32),
                    pltpu.SemaphoreType.DMA((len(arrived),)),
                    pltpu.SemaphoreType.DMA((WIN,)),
                ],
                compiler_params=params,
                name="cut_pieces",
            )(table, *arrived)
            pieces[1, step] = cut[1]
            wide_now = [cut[at] for at in moving]
            keys_now = [(at, step) for at in moving]

    buffers = [pieces[at, step] for step in range(last) for at in range(WIN)] + arrived
    updated = pl.pallas_call(
        functools.partial(
            finish_kernel, (species, levels, columns, tiles, static, narrow_count)
        ),
        in_specs=[smem] + [hbm] * len(buffers),
        out_specs=hbm,
        out_shape=jax.ShapeDtypeStruct((species, levels, columns), jnp.float32),
        scratch_shapes=[
            pltpu.VMEM((pair_total - WIN, piece) + row_shape, jnp.float32),
            pltpu.VMEM((3 * static,) + row_shape, jnp.float32),
            pltpu.VMEM((tiles, columns + 8, LANES), jnp.float32),
            pltpu.VMEM((species, levels, columns), jnp.float32),
            pltpu.SemaphoreType.DMA((len(buffers),)),
            pltpu.SemaphoreType.DMA((columns // LANES,)),
        ],
        compiler_params=params,
        name="place_columns",
    )(table, *buffers)
    return updated.transpose(1, 0, 2)


def solution(mesh):
    placed = (
        P(None, None, ("wide", "narrow")),
        P(("wide", "narrow")),
        P(),
        P(),
        P(("wide", "narrow")),
        P(("wide", "narrow")),
    )
    return jax.shard_map(
        local,
        mesh=mesh,
        in_specs=placed,
        out_specs=P(None, None, ("wide", "narrow")),
        check_vma=False,
    )
```

time: 405 us -> 407 us (level)
  loops' own time: 118 us -> 0.08 us
  waiting for transfers between devices: 161 us -> 272 us
  local copies, waits for them, and re-layouts: 39 us -> 16 us
  starting transfers between devices: 19.9 us -> 37.9 us
  Pallas kernels: 68.6 us -> 81.8 us
    another operation x15 -> x3, loops' own time: 118 us -> 0.08 us  [step_over(): return lax.switch(units_over(table[3, step * WIN], static), leaves, *parts)]
    ppermute x15 -> x18, waiting for transfers between devices: 161 us -> 272 us  [from_behind(): return lax.ppermute(value, axis, pairs)]
    ppermute x15 -> x18, starting transfers between devices: 19.9 us -> 37.9 us  [from_behind(): return lax.ppermute(value, axis, pairs)]
    dynamic_slice x6 -> x0, local copies, waits for them, and re-layouts: 11.6 us -> none  [the longest x3 6.88 us: branch(): part = lax.dynamic_slice_in_dim(moves[2 * at], moves[2 * at + 1], piece, 0)]
    pad x3 -> x0, local copies, waits for them, and re-layouts: 8.8 us -> none  [branch(): arrived = jnp.pad(arrived, ((0, spare), (0, 0), (0, 0), (0, 0)))]
    dynamic_update_slice x4 -> x0, local copies, waits for them, and re-layouts: 8.64 us -> none  [local(): lax.dynamic_update_slice_in_dim(merged, early[at], inner(last, at), 0)]
    another operation x1 -> x12, local copies, waits for them, and re-layouts: 2.44 us -> 9.44 us
    pallas_call x1 -> x5, Pallas kernels: 45.6 us -> 52 us  [the longest x3 43.8 us: integrate(): pl.pallas_call(functools.partial(integrate_kernel, (levels, pad, tiles),...]
  transfers between devices with their start and end apart: 15 -> 18, of which waited for: 7 -> 15; matrix products, arithmetic and copies ran while one was open for 4% -> 0% of each run, Pallas kernels for 0% -> 5%
where the time goes in v1:
time: 407 us; the launch traced here: 411 us
  waiting for transfers between devices  272 us (67%)
  Pallas kernels  81.8 us (20%)
  starting transfers between devices  37.9 us (9%)
  local copies, waits for them, and re-layouts  16 us (4%)
    ppermute x18, waiting for transfers between devices, from_behind(): return lax.ppermute(value, axis, pairs)  272 us
    pallas_call x3, Pallas kernels, integrate(): pl.pallas_call(functools.partial(integrate_kernel, (levels, pad, tiles),...  43.8 us
    ppermute x18, starting transfers between devices, from_behind(): return lax.ppermute(value, axis, pairs)  37.9 us
    pallas_call x1, Pallas kernels, local(): pl.pallas_call(functools.partial(sort_kernel, (species, levels, columns,...  19.6 us
    pallas_call x1, Pallas kernels, local(): pl.pallas_call(functools.partial(finish_kernel, (species, levels, columns...  10.2 us
    another operation x12, local copies, waits for them, and re-layouts  9.44 us
    pallas_call x2, Pallas kernels, local(): pl.pallas_call(functools.partial(cut_kernel, static, step), in_specs=[sme...  8.26 us
  transfers between devices with their start and end apart: 18, of which 15 were waited for; matrix products, arithmetic and copies ran while one was open for 0% of the time, Pallas kernels for 5%

profile of v1, /device:TPU:0, one launch (start us, length us, event | category | flops | bytes accessed | tf_op | source)
XLA Modules:
  0.0 411.0 jit_solution(4136031732768190964)
XLA Ops:
  0.7 19.6 %sort_columns.1 = (f32[448,7,8,128]{3,2,1,0:T(8,128)}, s32[8,128]{1,0:T(8,128)}, f32[64,7,8,128]{3,2,1,0:T(8,128)}, f32[4,7,8,128]{3,2,1,0:T(8,128)S(1)}, f32[32...) custom-call(s32[2]{0:T(128)} %pad_add_fusion.me_ref, ...), custom_call_target="tpu_custom_call" | custom-call | tf_op jit(solution)/shard_map/sort_columns/pallas_call | solution.py:408
  23.2 13.8 %integrate_columns.4 = (f32[64,7,8,128]{3,2,1,0:T(8,128)}, f32[4,7,8,128]{3,2,1,0:T(8,128)S(1)}, f32[32,7,8,128]{3,2,1,0:T(8,128)S(1)}, f32[16,7,8,128]{3,2,1,0:...) custom-call(s32[8,128]{1,0:T(8,128)} %get-tuple-element.488.table_ref, ...), custom_call_target="tpu_custom_call" | custom-call | flops 3082813440 | bytes 12845056 | tf_op jit(solution)/shard_map/integrate_columns/pallas_call | solution.py:447
  38.3 3.8 conditional.4
  42.2 3.8 conditional.3
  46.0 6.3 %collective-permute-start.144 = (f32[32,7,8,128]{3,2,1,0:T(8,128)}, f32[32,7,8,128]{3,2,1,0:T(8,128)S(1)}, u32[]{:S(2)}, u32[]{:S(2)}) collective-permute-start(f32[32,7,8,128]{3,2,1,0:T(8,128)} %get-tuple-element.489), channel_id=1, source_target_pairs={{0,28},{4,0},{8,4},{12,8},{16,12},{20,16},{24,20},{28,24},{1,29},{... | collective-permute-start | bytes 2752520 | tf_op jit(solution)/shard_map/ppermute | solution.py:22
  52.3 3.6 collective-permute-start.147
  56.2 17.2 %collective-permute-done.144.refs_0_ = f32[32,7,8,128]{3,2,1,0:T(8,128)S(1)} collective-permute-done((f32[32,7,8,128]{3,2,1,0:T(8,128)}, f32[32,7,8,128]{3,2,1,0:T(8,128)S(1)}, u32[]{:S(2)}, u32[]{:S(2)}) %collective-permute-start.144) | collective-permute-done | bytes 917536 | tf_op jit(solution)/shard_map/ppermute | solution.py:22
  76.9 20.0 %collective-permute-done.146.refs_2_ = f32[32,7,8,128]{3,2,1,0:T(8,128)S(1)} collective-permute-done((f32[32,7,8,128]{3,2,1,0:T(8,128)}, f32[32,7,8,128]{3,2,1,0:T(8,128)S(1)}, u32[]{:S(2)}, u32[]{:S(2)}) %collective-permute-start.146) | collective-permute-done | bytes 917536 | tf_op jit(solution)/shard_map/ppermute | solution.py:22
  96.9 15.8 %collective-permute-done.147.refs_4_ = f32[32,7,8,128]{3,2,1,0:T(8,128)S(1)} collective-permute-done((f32[32,7,8,128]{3,2,1,0:T(8,128)}, f32[32,7,8,128]{3,2,1,0:T(8,128)S(1)}, u32[]{:S(2)}, u32[]{:S(2)}) %collective-permute-start.147) | collective-permute-done | bytes 917536 | tf_op jit(solution)/shard_map/ppermute | solution.py:22
  116.3 19.8 %collective-permute-done.149.refs_6_ = f32[32,7,8,128]{3,2,1,0:T(8,128)} collective-permute-done((f32[32,7,8,128]{3,2,1,0:T(8,128)}, f32[32,7,8,128]{3,2,1,0:T(8,128)}, u32[]{:S(2)}, u32[]{:S(2)}) %collective-permute-start.149) | collective-permute-done | bytes 917536 | tf_op jit(solution)/shard_map/ppermute | solution.py:22
  136.2 17.8 %integrate_columns.3 = (f32[64,7,8,128]{3,2,1,0:T(8,128)}, f32[4,7,8,128]{3,2,1,0:T(8,128)}, f32[32,7,8,128]{3,2,1,0:T(8,128)}, f32[16,7,8,128]{3,2,1,0:T(8,128)...) custom-call(s32[8,128]{1,0:T(8,128)} %get-tuple-element.488.table_re, ...), custom_call_target="tpu_custom_call" | custom-call | flops 4315938816 | bytes 23855104 | tf_op jit(solution)/shard_map/integrate_columns/pallas_call | solution.py:447
  154.0 21.2 %conditional.5 = (f32[4,7,8,128]{3,2,1,0:T(8,128)}, f32[32,7,8,128]{3,2,1,0:T(8,128)}, f32[16,7,8,128]{3,2,1,0:T(8,128)}, f32[8,7,8,128]{3,2,1,0:T(8,128)}, f32[4,7,8,128]{3,2,1,0:T(8,128)}) conditional(s32[]{:T(128)} %bitcast.9, () %tuple.241, f32[4,7,8,128]{3,2,1,0:T(8,128)} %get-tuple-element.535, ...), branch_computations={%region_34.35_spmd, %region_35.36_spmd, %region_36.37_spmd, %regio... | conditional | bytes 7340272 | solution.py:495
  154.0 3.7 collective-permute-start.107
  158.3 12.6 %collective-permute-done.106 = f32[4,7,8,128]{3,2,1,0:T(8,128)} collective-permute-done((f32[4,7,8,128]{3,2,1,0:T(8,128)}, f32[4,7,8,128]{3,2,1,0:T(8,128)}, u32[]{:S(2)}, u32[]{:S(2)}) %collective-permute-start.106) | collective-permute-done | bytes 114720 | tf_op jit(solution)/shard_map/cond/branch_6_fun/ppermute | solution.py:22
  180.0 117.3 %collective-permute-done.154.refs_0_ = f32[64,7,8,128]{3,2,1,0:T(8,128)S(1)} collective-permute-done((f32[64,7,8,128]{3,2,1,0:T(8,128)}, f32[64,7,8,128]{3,2,1,0:T(8,128)S(1)}, u32[]{:S(2)}, u32[]{:S(2)}) %collective-permute-start.154) | collective-permute-done | bytes 1835040 | tf_op jit(solution)/shard_map/ppermute | solution.py:22
  298.5 4.1 %cut_pieces.3 = (f32[32,7,8,128]{3,2,1,0:T(8,128)}, f32[32,7,8,128]{3,2,1,0:T(8,128)}, f32[32,7,8,128]{3,2,1,0:T(8,128)}, f32[32,7,8,128]{3,2,1,0:T(8,128)}) custom-call(s32[8,128]{1,0:T(8,128)} %get-tuple-element.488.table_ref, f32[64,7,8,128]{3,2,1,0:T(8,128)} %copy-done.2, f32[4,7,8,128]{3,2,1,0:T(8,128)} %get-tuple-element.521.refs_1_, ...), custom_call_target="tpu_custom_call" | custom-call | tf_op jit(solution)/shard_map/cut_pieces/pallas_call | solution.py:554
  302.6 15.9 %collective-permute-start.155 = (f32[32,7,8,128]{3,2,1,0:T(8,128)}, f32[32,7,8,128]{3,2,1,0:T(8,128)}, u32[]{:S(2)}, u32[]{:S(2)}) collective-permute-start(f32[32,7,8,128]{3,2,1,0:T(8,128)} %get-tuple-element.526), channel_id=1, source_target_pairs={{0,28},{4,0},{8,4},{12,8},{16,12},{20,16},{24,20},{28,24},{1,29},{... | collective-permute-start | bytes 2752520 | tf_op jit(solution)/shard_map/ppermute | solution.py:22
  319.7 4.1 %cut_pieces.2 = (f32[32,7,8,128]{3,2,1,0:T(8,128)}, f32[32,7,8,128]{3,2,1,0:T(8,128)}, f32[32,7,8,128]{3,2,1,0:T(8,128)}, f32[32,7,8,128]{3,2,1,0:T(8,128)}) custom-call(s32[8,128]{1,0:T(8,128)} %get-tuple-element.488.table_ref, f32[64,7,8,128]{3,2,1,0:T(8,128)} %copy-done.1, f32[4,7,8,128]{3,2,1,0:T(8,128)} %get-tuple-element.506.refs_1_, ...), custom_call_target="tpu_custom_call" | custom-call | tf_op jit(solution)/shard_map/cut_pieces/pallas_call | solution.py:554
  326.6 12.4 %collective-permute-done.155.refs_0_ = f32[32,7,8,128]{3,2,1,0:T(8,128)} collective-permute-done((f32[32,7,8,128]{3,2,1,0:T(8,128)}, f32[32,7,8,128]{3,2,1,0:T(8,128)}, u32[]{:S(2)}, u32[]{:S(2)}) %collective-permute-start.155) | collective-permute-done | bytes 917536 | tf_op jit(solution)/shard_map/ppermute | solution.py:22
  342.3 17.7 %collective-permute-done.157.refs_3_ = f32[32,7,8,128]{3,2,1,0:T(8,128)} collective-permute-done((f32[32,7,8,128]{3,2,1,0:T(8,128)}, f32[32,7,8,128]{3,2,1,0:T(8,128)}, u32[]{:S(2)}, u32[]{:S(2)}) %collective-permute-start.157) | collective-permute-done | bytes 917536 | tf_op jit(solution)/shard_map/ppermute | solution.py:22
  360.1 12.1 %integrate_columns.5 = (f32[32,7,8,128]{3,2,1,0:T(8,128)}, f32[32,7,8,128]{3,2,1,0:T(8,128)}, f32[32,7,8,128]{3,2,1,0:T(8,128)}, f32[32,7,8,128]{3,2,1,0:T(8,128)}) custom-call(s32[8,128]{1,0:T(8,128)} %get-tuple-element.488.table_ref, f32[224,1]{1,0:T(8,128)} %copy.7.loss_ref, bf16[224,224]{1,0:T(8,128)(2,1)} %pad.9.coupling_ref, ...), custom_call_target="tpu_custom_call" | custom-call | flops 2466250752 | bytes 11010048 | tf_op jit(solution)/shard_map/integrate_columns/pallas_call | solution.py:447
  372.2 6.1 %collective-permute-done.151.refs_4_ = f32[32,7,8,128]{3,2,1,0:T(8,128)S(1)} collective-permute-done((f32[32,7,8,128]{3,2,1,0:T(8,128)}, f32[32,7,8,128]{3,2,1,0:T(8,128)S(1)}, u32[]{:S(2)}, u32[]{:S(2)}) %collective-permute-start.151) | collective-permute-done | bytes 917536 | tf_op jit(solution)/shard_map/ppermute | solution.py:22
  381.5 17.9 %collective-permute-done.153.refs_7_ = f32[32,7,8,128]{3,2,1,0:T(8,128)} collective-permute-done((f32[32,7,8,128]{3,2,1,0:T(8,128)}, f32[32,7,8,128]{3,2,1,0:T(8,128)}, u32[]{:S(2)}, u32[]{:S(2)}) %collective-permute-start.153) | collective-permute-done | bytes 917536 | tf_op jit(solution)/shard_map/ppermute | solution.py:22
  400.6 10.2 %place_columns.1 = f32[221,4,2048]{2,1,0:T(4,128)} custom-call(s32[8,128]{1,0:T(8,128)} %get-tuple-element.488.table_ref, f32[32,7,8,128]{3,2,1,0:T(8,128)} %get-tuple-element.496.refs_0_, f32[32,7,8,128]{3,2,1,0:T(8,128)} %get-tuple-element.497.refs_1_, f32[32,7,8,128]{3,2,1,0:T(8,128)} %get-tuple-element.498.refs_2_, ...), custom_call_target="tpu_custom_call" | custom-call | tf_op jit(solution)/shard_map/place_columns/pallas_call | solution.py:572
  (63 shorter events, 40.5 us)
Async XLA Ops:
  0.7 21.9 %copy-start.9 = (bf16[221,221]{1,0:T(8,128)(2,1)S(1)}, bf16[221,221]{1,0:T(8,128)(2,1)}, u32[]{:S(2)}) copy-start(bf16[221,221]{1,0:T(8,128)(2,1)} %param.60) | copy-start | bytes 293050
  46.0 27.4 %collective-permute-start.144 = (f32[32,7,8,128]{3,2,1,0:T(8,128)}, f32[32,7,8,128]{3,2,1,0:T(8,128)S(1)}, u32[]{:S(2)}, u32[]{:S(2)}) collective-permute-start(f32[32,7,8,128]{3,2,1,0:T(8,128)} %get-tuple-element.489), channel_id=1, source_target_pairs={{0,28},{4,0},{8,4},{12,8},{16,12},{20,16},{24,20},{28,24},{1,29},{... | collective-permute-start | bytes 2752520 | tf_op jit(solution)/shard_map/ppermute | solution.py:22
  52.3 24.6 %collective-permute-start.145 = (f32[32,7,8,128]{3,2,1,0:T(8,128)}, f32[32,7,8,128]{3,2,1,0:T(8,128)S(1)}, u32[]{:S(2)}, u32[]{:S(2)}) collective-permute-start(f32[32,7,8,128]{3,2,1,0:T(8,128)} %get-tuple-element.490), channel_id=1, source_target_pairs={{0,4},{4,8},{8,12},{12,16},{16,20},{20,24},{24,28},{28,0},{1,5},{5... | collective-permute-start | bytes 2752520 | tf_op jit(solution)/shard_map/ppermute | solution.py:22
  52.3 44.6 %collective-permute-start.146 = (f32[32,7,8,128]{3,2,1,0:T(8,128)}, f32[32,7,8,128]{3,2,1,0:T(8,128)S(1)}, u32[]{:S(2)}, u32[]{:S(2)}) collective-permute-start(f32[32,7,8,128]{3,2,1,0:T(8,128)} %get-tuple-element.491), channel_id=1, source_target_pairs={{0,8},{4,12},{8,16},{12,20},{16,24},{20,28},{24,0},{28,4},{1,9},{5... | collective-permute-start | bytes 2752520 | tf_op jit(solution)/shard_map/ppermute | solution.py:22
  52.3 60.4 %collective-permute-start.147 = (f32[32,7,8,128]{3,2,1,0:T(8,128)}, f32[32,7,8,128]{3,2,1,0:T(8,128)S(1)}, u32[]{:S(2)}, u32[]{:S(2)}) collective-permute-start(f32[32,7,8,128]{3,2,1,0:T(8,128)} %get-tuple-element.493), channel_id=1, source_target_pairs={{0,28},{4,0},{8,4},{12,8},{16,12},{20,16},{24,20},{28,24},{1,29},{... | collective-permute-start | bytes 2752520 | tf_op jit(solution)/shard_map/ppermute | solution.py:22
  55.9 60.4 %collective-permute-start.148 = (f32[32,7,8,128]{3,2,1,0:T(8,128)}, f32[32,7,8,128]{3,2,1,0:T(8,128)}, u32[]{:S(2)}, u32[]{:S(2)}) collective-permute-start(f32[32,7,8,128]{3,2,1,0:T(8,128)} %get-tuple-element.494), channel_id=1, source_target_pairs={{0,4},{4,8},{8,12},{12,16},{16,20},{20,24},{24,28},{28,0},{1,5},{5... | collective-permute-start | bytes 2752520 | tf_op jit(solution)/shard_map/ppermute | solution.py:22
  73.4 62.7 %copy-start.3 = (f32[32,7,8,128]{3,2,1,0:T(8,128)}, f32[32,7,8,128]{3,2,1,0:T(8,128)S(1)}, u32[]{:S(2)}) copy-start(f32[32,7,8,128]{3,2,1,0:T(8,128)S(1)} %collective-permute-done.144.refs_0_) | copy-start | bytes 2752516
  73.4 62.7 %collective-permute-start.149 = (f32[32,7,8,128]{3,2,1,0:T(8,128)}, f32[32,7,8,128]{3,2,1,0:T(8,128)}, u32[]{:S(2)}, u32[]{:S(2)}) collective-permute-start(f32[32,7,8,128]{3,2,1,0:T(8,128)} %get-tuple-element.495), channel_id=1, source_target_pairs={{0,8},{4,12},{8,16},{12,20},{16,24},{20,28},{24,0},{28,4},{1,9},{5... | collective-permute-start | bytes 2752520 | tf_op jit(solution)/shard_map/ppermute | solution.py:22
  76.9 59.3 %copy-start.4 = (f32[32,7,8,128]{3,2,1,0:T(8,128)}, f32[32,7,8,128]{3,2,1,0:T(8,128)S(1)}, u32[]{:S(2)}) copy-start(f32[32,7,8,128]{3,2,1,0:T(8,128)S(1)} %collective-permute-done.145.refs_1_) | copy-start | bytes 2752516
  96.9 39.3 %copy-start.6 = (f32[32,7,8,128]{3,2,1,0:T(8,128)}, f32[32,7,8,128]{3,2,1,0:T(8,128)S(1)}, u32[]{:S(2)}) copy-start(f32[32,7,8,128]{3,2,1,0:T(8,128)S(1)} %collective-permute-done.146.refs_2_) | copy-start | bytes 2752516
  112.7 23.4 %copy-start.7 = (f32[32,7,8,128]{3,2,1,0:T(8,128)}, f32[32,7,8,128]{3,2,1,0:T(8,128)S(1)}, u32[]{:S(2)}) copy-start(f32[32,7,8,128]{3,2,1,0:T(8,128)S(1)} %collective-permute-done.147.refs_4_) | copy-start | bytes 2752516
  154.0 19.3 %collective-permute-start.107 = (f32[16,7,8,128]{3,2,1,0:T(8,128)S(1)}, f32[16,7,8,128]{3,2,1,0:T(8,128)}, u32[]{:S(2)}, u32[]{:S(2)}) collective-permute-start(f32[16,7,8,128]{3,2,1,0:T(8,128)S(1)} %get-tuple-element.394), channel_id=1, source_target_pairs={{0,3},{1,0},{2,1},{3,2},{4,7},{5,4},{6,5},{7,6},{8,11},{9,8},{10,9... | collective-permute-start | bytes 1376264 | tf_op jit(solution)/shard_map/cond/branch_6_fun/ppermute | solution.py:22
  157.7 13.2 %collective-permute-start.106 = (f32[4,7,8,128]{3,2,1,0:T(8,128)}, f32[4,7,8,128]{3,2,1,0:T(8,128)}, u32[]{:S(2)}, u32[]{:S(2)}) collective-permute-start(f32[4,7,8,128]{3,2,1,0:T(8,128)} %get-tuple-element.393), channel_id=1, source_target_pairs={{0,3},{1,0},{2,1},{3,2},{4,7},{5,4},{6,5},{7,6},{8,11},{9,8},{10,9... | collective-permute-start | bytes 344072 | tf_op jit(solution)/shard_map/cond/branch_6_fun/ppermute | solution.py:22
  158.1 15.2 %collective-permute-start.108 = (f32[4,7,8,128]{3,2,1,0:T(8,128)}, f32[4,7,8,128]{3,2,1,0:T(8,128)}, u32[]{:S(2)}, u32[]{:S(2)}) collective-permute-start(f32[4,7,8,128]{3,2,1,0:T(8,128)} %get-tuple-element.395), channel_id=1, source_target_pairs={{0,3},{1,0},{2,1},{3,2},{4,7},{5,4},{6,5},{7,6},{8,11},{9,8},{10,9... | collective-permute-start | bytes 344072 | tf_op jit(solution)/shard_map/cond/branch_6_fun/ppermute | solution.py:22
  175.1 122.1 %collective-permute-start.154 = (f32[64,7,8,128]{3,2,1,0:T(8,128)}, f32[64,7,8,128]{3,2,1,0:T(8,128)S(1)}, u32[]{:S(2)}, u32[]{:S(2)}) collective-permute-start(f32[64,7,8,128]{3,2,1,0:T(8,128)} %get-tuple-element.515), channel_id=1, source_target_pairs={{0,2},{1,3},{2,0},{3,1},{4,6},{5,7},{6,4},{7,5},{8,10},{9,11},{10,... | collective-permute-start | bytes 5505032 | tf_op jit(solution)/shard_map/ppermute | solution.py:22
  176.6 141.9 %collective-permute-start.150 = (f32[64,7,8,128]{3,2,1,0:T(8,128)}, f32[64,7,8,128]{3,2,1,0:T(8,128)S(1)}, u32[]{:S(2)}, u32[]{:S(2)}) collective-permute-start(f32[64,7,8,128]{3,2,1,0:T(8,128)} %get-tuple-element.500), channel_id=1, source_target_pairs={{0,1},{1,2},{2,3},{3,0},{4,5},{5,6},{6,7},{7,4},{8,9},{9,10},{10,1... | collective-permute-start | bytes 5505032 | tf_op jit(solution)/shard_map/ppermute | solution.py:22
  302.6 36.4 %collective-permute-start.155 = (f32[32,7,8,128]{3,2,1,0:T(8,128)}, f32[32,7,8,128]{3,2,1,0:T(8,128)}, u32[]{:S(2)}, u32[]{:S(2)}) collective-permute-start(f32[32,7,8,128]{3,2,1,0:T(8,128)} %get-tuple-element.526), channel_id=1, source_target_pairs={{0,28},{4,0},{8,4},{12,8},{16,12},{20,16},{24,20},{28,24},{1,29},{... | collective-permute-start | bytes 2752520 | tf_op jit(solution)/shard_map/ppermute | solution.py:22
  318.5 23.9 %collective-permute-start.156 = (f32[32,7,8,128]{3,2,1,0:T(8,128)}, f32[32,7,8,128]{3,2,1,0:T(8,128)}, u32[]{:S(2)}, u32[]{:S(2)}) collective-permute-start(f32[32,7,8,128]{3,2,1,0:T(8,128)} %get-tuple-element.528), channel_id=1, source_target_pairs={{0,4},{4,8},{8,12},{12,16},{16,20},{20,24},{24,28},{28,0},{1,5},{5... | collective-permute-start | bytes 2752520 | tf_op jit(solution)/shard_map/ppermute | solution.py:22
  318.5 80.9 %collective-permute-start.158 = (f32[64,7,8,128]{3,2,1,0:T(8,128)}, f32[64,7,8,128]{3,2,1,0:T(8,128)S(1)}, u32[]{:S(2)}, u32[]{:S(2)}) collective-permute-start(f32[64,7,8,128]{3,2,1,0:T(8,128)} %get-tuple-element.534), channel_id=1, source_target_pairs={{0,3},{1,0},{2,1},{3,2},{4,7},{5,4},{6,5},{7,6},{8,11},{9,8},{10,9... | collective-permute-start | bytes 5505032 | tf_op jit(solution)/shard_map/ppermute | solution.py:22
  318.5 41.6 %collective-permute-start.157 = (f32[32,7,8,128]{3,2,1,0:T(8,128)}, f32[32,7,8,128]{3,2,1,0:T(8,128)}, u32[]{:S(2)}, u32[]{:S(2)}) collective-permute-start(f32[32,7,8,128]{3,2,1,0:T(8,128)} %get-tuple-element.529), channel_id=1, source_target_pairs={{0,8},{4,12},{8,16},{12,20},{16,24},{20,28},{24,0},{28,4},{1,9},{5... | collective-permute-start | bytes 2752520 | tf_op jit(solution)/shard_map/ppermute | solution.py:22
  323.9 54.4 %collective-permute-start.151 = (f32[32,7,8,128]{3,2,1,0:T(8,128)}, f32[32,7,8,128]{3,2,1,0:T(8,128)S(1)}, u32[]{:S(2)}, u32[]{:S(2)}) collective-permute-start(f32[32,7,8,128]{3,2,1,0:T(8,128)} %get-tuple-element.511), channel_id=1, source_target_pairs={{0,28},{4,0},{8,4},{12,8},{16,12},{20,16},{24,20},{28,24},{1,29},{... | collective-permute-start | bytes 2752520 | tf_op jit(solution)/shard_map/ppermute | solution.py:22
  339.0 42.5 %collective-permute-start.152 = (f32[32,7,8,128]{3,2,1,0:T(8,128)}, f32[32,7,8,128]{3,2,1,0:T(8,128)S(1)}, u32[]{:S(2)}, u32[]{:S(2)}) collective-permute-start(f32[32,7,8,128]{3,2,1,0:T(8,128)} %get-tuple-element.513), channel_id=1, source_target_pairs={{0,4},{4,8},{8,12},{12,16},{16,20},{20,24},{24,28},{28,0},{1,5},{5... | collective-permute-start | bytes 2752520 | tf_op jit(solution)/shard_map/ppermute | solution.py:22
  342.3 57.1 %collective-permute-start.153 = (f32[32,7,8,128]{3,2,1,0:T(8,128)}, f32[32,7,8,128]{3,2,1,0:T(8,128)}, u32[]{:S(2)}, u32[]{:S(2)}) collective-permute-start(f32[32,7,8,128]{3,2,1,0:T(8,128)} %get-tuple-element.514), channel_id=1, source_target_pairs={{0,8},{4,12},{8,16},{12,20},{16,24},{20,28},{24,0},{28,4},{1,9},{5... | collective-permute-start | bytes 2752520 | tf_op jit(solution)/shard_map/ppermute | solution.py:22
  378.3 21.1 %copy-start.5 = (f32[32,7,8,128]{3,2,1,0:T(8,128)}, f32[32,7,8,128]{3,2,1,0:T(8,128)S(1)}, u32[]{:S(2)}) copy-start(f32[32,7,8,128]{3,2,1,0:T(8,128)S(1)} %collective-permute-done.151.refs_4_) | copy-start | bytes 2752516
  (6 other events, 56.3 us)
